TPU v7x, 32 devices: a whole 2x2x4 slice. The times are simulated.
32 devices in a mesh: groups: 2 (over x), blk: 16 (over z, y, core).
Axes of the slice: x: 2, y: 2, z: 4, core: 2. Of those that a mesh axis runs over, the one named last changes fastest.
Arguments:
- queries: bfloat16 [4096, 512], P(('groups', 'blk')), parts along dimension 0, may hold values from -8 to 8
- key_states: bfloat16 [4096, 128], P(('groups', 'blk')), parts along dimension 0, may hold values from -6 to 6
- value_states: bfloat16 [4096, 128], P(('groups', 'blk')), parts along dimension 0, may hold values from -6 to 6
- grad_out: bfloat16 [4096, 512], P(('groups', 'blk')), parts along dimension 0, may hold values from -6 to 6
- tile_mask: int32 [32, 16], P('groups'), parts along dimension 0, may hold values 0 or 1
- block_order: int32 [32], P('groups'), parts along dimension 0, may hold values from 0 to 15, each once
Outputs:
- attended: bfloat16 [4096, 512], P(('groups', 'blk')), parts along dimension 0
- grad_queries: bfloat16 [4096, 512], P(('groups', 'blk')), parts along dimension 0
- grad_keys: float32 [4096, 128], P(('groups', 'blk')), parts along dimension 0
- grad_values: float32 [4096, 128], P(('groups', 'blk')), parts along dimension 0
There are 2 independent parts, one for each index of `groups`. A program takes and returns all parts, laid end to end along the dimension named above; each array names one. Nothing has to cross between parts.
Inputs may be any that keep to these rules, and one draw needn't show every extreme that they name: `block_order`: each block number appears once.
All inputs are finite; a program needn't handle non-finite values.
Results may differ from a plain program's by a relative error of at most 0.04.
Values may be sent and summed in bfloat16 or wider, within the bound.
A program may use at most 64 MiB of HBM per device.

v0:
```python
import jax
import jax.numpy as jnp
from jax import lax
from jax.sharding import PartitionSpec as P

TILE = 128


def passed_along(value, axis, steps):
    count = lax.axis_size(axis)
    pairs = [(source, (source + steps) % count) for source in range(count)]
    return lax.ppermute(value, axis, pairs)


def shards(queries, key_states, value_states, grad_out, tile_mask, block_order):
    cycle_size = lax.axis_size("blk")
    my_index = lax.axis_index("blk")
    tok_rows = key_states.shape[0]
    head_width = key_states.shape[1]
    head_count = queries.shape[1] // head_width
    scaling = head_width ** (-0.5)
    tiles_per = tok_rows // TILE
    tile_total = tile_mask.shape[1]
    offsets = jnp.arange(tok_rows, dtype=jnp.int32)
    my_block = block_order[my_index]
    total_rows = head_count * tok_rows

    def to_rows(features):
        return (
            features.reshape(tok_rows, head_count, head_width)
            .transpose(1, 0, 2)
            .reshape(total_rows, head_width)
        )

    def from_rows(row_form):
        return (
            row_form.reshape(head_count, tok_rows, head_width)
            .transpose(1, 0, 2)
            .reshape(tok_rows, head_count * head_width)
        )

    query_rows = to_rows(queries)
    cot_rows = to_rows(grad_out)

    def mask_for(query_block, key_pos):
        query_pos = query_block * tok_rows + offsets
        tile_rows = lax.dynamic_slice_in_dim(
            tile_mask, query_block * tiles_per, tiles_per, 0
        ).astype(jnp.float32)
        tile_rows = jnp.repeat(tile_rows, TILE, axis=0)
        one_hot = (
            (key_pos // TILE)[:, None] == jnp.arange(tile_total, dtype=jnp.int32)[None, :]
        ).astype(jnp.float32)
        tile_bits = jnp.dot(tile_rows, one_hot.T, preferred_element_type=jnp.float32) > 0.5
        same_tile = (query_pos // TILE)[:, None] == (key_pos // TILE)[None, :]
        allowed = (query_pos[:, None] >= key_pos[None, :]) & (tile_bits | same_tile)
        return jnp.tile(allowed, (head_count, 1))

    def softmax_update(carry_state, key_sub, value_sub, allowed):
        run_max, run_sum, run_acc = carry_state
        scores = (
            jnp.einsum("rd,kd->rk", query_rows, key_sub, preferred_element_type=jnp.float32)
            * scaling
        )
        scores = jnp.where(allowed, scores, -1e30)
        new_max = jnp.maximum(run_max, jnp.max(scores, axis=1))
        weights = jnp.where(allowed, jnp.exp(scores - new_max[:, None]), 0.0)
        factor = jnp.exp(run_max - new_max)
        run_sum = run_sum * factor + jnp.sum(weights, axis=1)
        run_acc = run_acc * factor[:, None] + jnp.dot(
            weights.astype(jnp.bfloat16), value_sub, preferred_element_type=jnp.float32
        )
        return (new_max, run_sum, run_acc)

    def guarded_update(carry_state, key_sub, value_sub, allowed):
        return softmax_update(carry_state, key_sub, value_sub, allowed)

    start_state = (
        jnp.full((total_rows,), -1e30, jnp.float32),
        jnp.zeros((total_rows,), jnp.float32),
        jnp.zeros((total_rows, head_width), jnp.float32),
    )
    key_piece = lax.all_gather(key_states, "blk", axis=0, tiled=True)
    value_piece = lax.all_gather(value_states, "blk", axis=0, tiled=True)
    piece_rows = key_piece.shape[0]

    def sub_step(sub_num, inner_state):
        first = sub_num * tok_rows
        key_sub = lax.dynamic_slice_in_dim(key_piece, first, tok_rows, 0)
        value_sub = lax.dynamic_slice_in_dim(value_piece, first, tok_rows, 0)
        key_ids = first + jnp.arange(tok_rows, dtype=jnp.int32)
        owners = key_ids // tok_rows
        owner_blocks = jnp.sum(
            jnp.where(
                owners[:, None] == jnp.arange(cycle_size, dtype=jnp.int32)[None, :],
                block_order[None, :],
                0,
            ),
            axis=1,
        )
        key_pos = owner_blocks * tok_rows + key_ids % tok_rows
        return guarded_update(inner_state, key_sub, value_sub, mask_for(my_block, key_pos))

    run_max, run_sum, run_acc = lax.fori_loop(0, piece_rows // tok_rows, sub_step, start_state)
    log_sum = run_max + jnp.log(run_sum)
    out_rows = (run_acc / run_sum[:, None]).astype(jnp.bfloat16)
    attended = from_rows(out_rows)
    row_delta = jnp.sum(cot_rows.astype(jnp.float32) * out_rows.astype(jnp.float32), axis=1)

    def block_grads(q_part, cot_part, sum_part, delta_part, key_sub, value_sub, allowed):
        scores = (
            jnp.einsum("rd,kd->rk", q_part, key_sub, preferred_element_type=jnp.float32) * scaling
        )
        weights = jnp.where(allowed, jnp.exp(scores - sum_part[:, None]), 0.0)
        value_term = jnp.einsum(
            "rk,rd->kd", weights.astype(jnp.bfloat16), cot_part, preferred_element_type=jnp.float32
        )
        d_prob = jnp.einsum("rd,kd->rk", cot_part, value_sub, preferred_element_type=jnp.float32)
        d_score = (weights * (d_prob - delta_part[:, None])).astype(jnp.bfloat16)
        query_term = jnp.dot(d_score, key_sub, preferred_element_type=jnp.float32) * scaling
        key_term = (
            jnp.einsum("rk,rd->kd", d_score, q_part, preferred_element_type=jnp.float32) * scaling
        )
        return (query_term, key_term, value_term)

    def guarded_grads(q_part, cot_part, sum_part, delta_part, key_sub, value_sub, allowed):
        return block_grads(q_part, cot_part, sum_part, delta_part, key_sub, value_sub, allowed)

    zero_keys = jnp.zeros((tok_rows, head_width), jnp.float32)
    zero_queries = jnp.zeros((total_rows, head_width), jnp.float32)

    def key_step(step_num, carry_state):
        key_cur, value_cur, key_acc, value_acc, query_acc = carry_state
        source = (my_index - step_num) % cycle_size
        key_pos = block_order[source] * tok_rows + offsets
        allowed = mask_for(my_block, key_pos)
        query_term, key_term, value_term = guarded_grads(
            query_rows, cot_rows, log_sum, row_delta, key_cur, value_cur, allowed
        )
        return (
            key_cur,
            value_cur,
            key_acc + key_term,
            value_acc + value_term,
            query_acc + query_term,
        )

    def key_turn(step_num, carry_state):
        key_cur, value_cur, key_acc, value_acc, query_acc = key_step(step_num, carry_state)
        key_cur, value_cur = passed_along((key_cur, value_cur), "blk", 1)
        key_acc, value_acc = passed_along((key_acc, value_acc), "blk", 1)
        return (key_cur, value_cur, key_acc, value_acc, query_acc)

    carry_state = (key_states, value_states, zero_keys, zero_keys, zero_queries)
    carry_state = lax.fori_loop(0, cycle_size - 1, key_turn, carry_state)
    carry_state = key_step(cycle_size - 1, carry_state)
    key_acc, value_acc = passed_along((carry_state[2], carry_state[3]), "blk", 1)
    query_acc = carry_state[4]
    grad_queries = from_rows(query_acc.astype(jnp.bfloat16))
    return (attended, grad_queries, key_acc, value_acc)


def solution(mesh):
    placed = (
        P(("groups", "blk"), None),
        P(("groups", "blk"), None),
        P(("groups", "blk"), None),
        P(("groups", "blk"), None),
        P("groups", None),
        P("groups"),
    )
    return jax.shard_map(
        shards,
        mesh=mesh,
        in_specs=placed,
        out_specs=(
            P(("groups", "blk"), None),
            P(("groups", "blk"), None),
            P(("groups", "blk"), None),
            P(("groups", "blk"), None),
        ),
        check_vma=False,
    )
```

profile of v0, /device:TPU:0, one launch (start us, length us, event | category | flops | bytes accessed | tf_op | source)
XLA Modules:
  0.0 222.9 jit_solution(3966216597943441637)
XLA Ops:
  0.7 0.8 copy.83
  6.8 24.6 %all_gather.6 = bf16[2048,128]{1,0:T(8,128)(2,1)S(1)} all-gather(bf16[128,128]{1,0:T(8,128)(2,1)S(1)} %copy.83), channel_id=1, replica_groups=mesh['groups'=2,'blk'=16] {'blk'}, dimensions={0}, use_global_device_ids=true | all-gather | bytes 557056 | tf_op jit(solution)/shard_map/all_gather | solution.py:83
  31.4 18.9 %all_gather.7 = bf16[2048,128]{1,0:T(8,128)(2,1)S(1)} all-gather(bf16[128,128]{1,0:T(8,128)(2,1)S(1)} %copy.84), channel_id=1, replica_groups=mesh['groups'=2,'blk'=16] {'blk'}, dimensions={0}, use_global_device_ids=true | all-gather | bytes 557056 | tf_op jit(solution)/shard_map/all_gather | solution.py:84
  50.2 17.7 %while.47 = (s32[]{:T(128)}, f32[512]{0:T(512)S(1)}, f32[512]{0:T(512)S(1)}, f32[512,128]{1,0:T(8,128)S(1)}, s32[]{:T(128)}, /*index=5*/s32[16]{0:T(128)S(1)}, b...) while((s32[]{:T(128)}, f32[512]{0:T(512)S(1)}, ...), condition=%wide.region_4.5_spmd.clone, body=%wide.region_0.4_spmd.clone.sunk | while | flops 34965508 | bytes 1841459 | solution.py:104
  69.2 144.8 %while.48 = (s32[]{:T(128)}, bf16[128,128]{1,0:T(8,128)(2,1)S(1)}, bf16[128,128]{1,0:T(8,128)(2,1)S(1)}, f32[128,128]{1,0:T(8,128)S(1)}, f32[128,128]{1,0:T(8,12...) while((s32[]{:T(128)}, bf16[128,128]{1,0:T(8,128)(2,1)S(1)}, ...), condition=%wide.region_7.8_spmd.clone.clone, body=%wide.region_6.7_spmd.clone.clone.sunk | while | flops 85202960 | bytes 3711538 | solution.py:155
  69.7 1.5 collective-permute-start.1
  74.4 0.9 collective-permute-done
  75.7 4.2 %collective-permute-done.2 = f32[128,128]{1,0:T(8,128)S(1)} collective-permute-done((f32[128,128]{1,0:T(8,128)S(1)}, f32[128,128]{1,0:T(8,128)S(1)}, u32[]{:S(2)}, u32[]{:S(2)}) %collective-permute-start.2) | collective-permute-done | bytes 65568 | tf_op jit(solution)/shard_map/while/body/eval_jaxpr/ppermute | solution.py:12
  79.9 0.7 collective-permute-done.3
  83.6 3.1 %collective-permute-done = bf16[128,128]{1,0:T(8,128)(2,1)S(1)} collective-permute-done((bf16[128,128]{1,0:T(8,128)(2,1)S(1)}, bf16[128,128]{1,0:T(8,128)(2,1)S(1)}, u32[]{:S(2)}, u32[]{:S(2)}) %collective-permute-start) | collective-permute-done | bytes 32800 | tf_op jit(solution)/shard_map/while/body/eval_jaxpr/ppermute | solution.py:12
  87.0 2.4 %collective-permute-done.2 = f32[128,128]{1,0:T(8,128)S(1)} collective-permute-done((f32[128,128]{1,0:T(8,128)S(1)}, f32[128,128]{1,0:T(8,128)S(1)}, u32[]{:S(2)}, u32[]{:S(2)}) %collective-permute-start.2) | collective-permute-done | bytes 65568 | tf_op jit(solution)/shard_map/while/body/eval_jaxpr/ppermute | solution.py:12
  89.4 0.7 collective-permute-done.3
  93.1 3.1 %collective-permute-done = bf16[128,128]{1,0:T(8,128)(2,1)S(1)} collective-permute-done((bf16[128,128]{1,0:T(8,128)(2,1)S(1)}, bf16[128,128]{1,0:T(8,128)(2,1)S(1)}, u32[]{:S(2)}, u32[]{:S(2)}) %collective-permute-start) | collective-permute-done | bytes 32800 | tf_op jit(solution)/shard_map/while/body/eval_jaxpr/ppermute | solution.py:12
  96.5 2.4 %collective-permute-done.2 = f32[128,128]{1,0:T(8,128)S(1)} collective-permute-done((f32[128,128]{1,0:T(8,128)S(1)}, f32[128,128]{1,0:T(8,128)S(1)}, u32[]{:S(2)}, u32[]{:S(2)}) %collective-permute-start.2) | collective-permute-done | bytes 65568 | tf_op jit(solution)/shard_map/while/body/eval_jaxpr/ppermute | solution.py:12
  98.9 0.7 collective-permute-done.3
  102.6 3.1 %collective-permute-done = bf16[128,128]{1,0:T(8,128)(2,1)S(1)} collective-permute-done((bf16[128,128]{1,0:T(8,128)(2,1)S(1)}, bf16[128,128]{1,0:T(8,128)(2,1)S(1)}, u32[]{:S(2)}, u32[]{:S(2)}) %collective-permute-start) | collective-permute-done | bytes 32800 | tf_op jit(solution)/shard_map/while/body/eval_jaxpr/ppermute | solution.py:12
  106.0 2.4 %collective-permute-done.2 = f32[128,128]{1,0:T(8,128)S(1)} collective-permute-done((f32[128,128]{1,0:T(8,128)S(1)}, f32[128,128]{1,0:T(8,128)S(1)}, u32[]{:S(2)}, u32[]{:S(2)}) %collective-permute-start.2) | collective-permute-done | bytes 65568 | tf_op jit(solution)/shard_map/while/body/eval_jaxpr/ppermute | solution.py:12
  112.2 3.1 %collective-permute-done = bf16[128,128]{1,0:T(8,128)(2,1)S(1)} collective-permute-done((bf16[128,128]{1,0:T(8,128)(2,1)S(1)}, bf16[128,128]{1,0:T(8,128)(2,1)S(1)}, u32[]{:S(2)}, u32[]{:S(2)}) %collective-permute-start) | collective-permute-done | bytes 32800 | tf_op jit(solution)/shard_map/while/body/eval_jaxpr/ppermute | solution.py:12
  115.6 2.4 %collective-permute-done.2 = f32[128,128]{1,0:T(8,128)S(1)} collective-permute-done((f32[128,128]{1,0:T(8,128)S(1)}, f32[128,128]{1,0:T(8,128)S(1)}, u32[]{:S(2)}, u32[]{:S(2)}) %collective-permute-start.2) | collective-permute-done | bytes 65568 | tf_op jit(solution)/shard_map/while/body/eval_jaxpr/ppermute | solution.py:12
  118.0 0.7 collective-permute-done.3
  121.7 3.1 %collective-permute-done = bf16[128,128]{1,0:T(8,128)(2,1)S(1)} collective-permute-done((bf16[128,128]{1,0:T(8,128)(2,1)S(1)}, bf16[128,128]{1,0:T(8,128)(2,1)S(1)}, u32[]{:S(2)}, u32[]{:S(2)}) %collective-permute-start) | collective-permute-done | bytes 32800 | tf_op jit(solution)/shard_map/while/body/eval_jaxpr/ppermute | solution.py:12
  125.1 2.4 %collective-permute-done.2 = f32[128,128]{1,0:T(8,128)S(1)} collective-permute-done((f32[128,128]{1,0:T(8,128)S(1)}, f32[128,128]{1,0:T(8,128)S(1)}, u32[]{:S(2)}, u32[]{:S(2)}) %collective-permute-start.2) | collective-permute-done | bytes 65568 | tf_op jit(solution)/shard_map/while/body/eval_jaxpr/ppermute | solution.py:12
  127.5 0.7 collective-permute-done.3
  131.2 3.1 %collective-permute-done = bf16[128,128]{1,0:T(8,128)(2,1)S(1)} collective-permute-done((bf16[128,128]{1,0:T(8,128)(2,1)S(1)}, bf16[128,128]{1,0:T(8,128)(2,1)S(1)}, u32[]{:S(2)}, u32[]{:S(2)}) %collective-permute-start) | collective-permute-done | bytes 32800 | tf_op jit(solution)/shard_map/while/body/eval_jaxpr/ppermute | solution.py:12
  134.6 2.4 %collective-permute-done.2 = f32[128,128]{1,0:T(8,128)S(1)} collective-permute-done((f32[128,128]{1,0:T(8,128)S(1)}, f32[128,128]{1,0:T(8,128)S(1)}, u32[]{:S(2)}, u32[]{:S(2)}) %collective-permute-start.2) | collective-permute-done | bytes 65568 | tf_op jit(solution)/shard_map/while/body/eval_jaxpr/ppermute | solution.py:12
  137.1 0.7 collective-permute-done.3
  140.8 3.1 %collective-permute-done = bf16[128,128]{1,0:T(8,128)(2,1)S(1)} collective-permute-done((bf16[128,128]{1,0:T(8,128)(2,1)S(1)}, bf16[128,128]{1,0:T(8,128)(2,1)S(1)}, u32[]{:S(2)}, u32[]{:S(2)}) %collective-permute-start) | collective-permute-done | bytes 32800 | tf_op jit(solution)/shard_map/while/body/eval_jaxpr/ppermute | solution.py:12
  144.2 2.4 %collective-permute-done.2 = f32[128,128]{1,0:T(8,128)S(1)} collective-permute-done((f32[128,128]{1,0:T(8,128)S(1)}, f32[128,128]{1,0:T(8,128)S(1)}, u32[]{:S(2)}, u32[]{:S(2)}) %collective-permute-start.2) | collective-permute-done | bytes 65568 | tf_op jit(solution)/shard_map/while/body/eval_jaxpr/ppermute | solution.py:12
  146.6 0.7 collective-permute-done.3
  150.3 3.1 %collective-permute-done = bf16[128,128]{1,0:T(8,128)(2,1)S(1)} collective-permute-done((bf16[128,128]{1,0:T(8,128)(2,1)S(1)}, bf16[128,128]{1,0:T(8,128)(2,1)S(1)}, u32[]{:S(2)}, u32[]{:S(2)}) %collective-permute-start) | collective-permute-done | bytes 32800 | tf_op jit(solution)/shard_map/while/body/eval_jaxpr/ppermute | solution.py:12
  153.7 2.4 %collective-permute-done.2 = f32[128,128]{1,0:T(8,128)S(1)} collective-permute-done((f32[128,128]{1,0:T(8,128)S(1)}, f32[128,128]{1,0:T(8,128)S(1)}, u32[]{:S(2)}, u32[]{:S(2)}) %collective-permute-start.2) | collective-permute-done | bytes 65568 | tf_op jit(solution)/shard_map/while/body/eval_jaxpr/ppermute | solution.py:12
  156.1 0.7 collective-permute-done.3
  159.8 3.1 %collective-permute-done = bf16[128,128]{1,0:T(8,128)(2,1)S(1)} collective-permute-done((bf16[128,128]{1,0:T(8,128)(2,1)S(1)}, bf16[128,128]{1,0:T(8,128)(2,1)S(1)}, u32[]{:S(2)}, u32[]{:S(2)}) %collective-permute-start) | collective-permute-done | bytes 32800 | tf_op jit(solution)/shard_map/while/body/eval_jaxpr/ppermute | solution.py:12
  163.2 2.4 %collective-permute-done.2 = f32[128,128]{1,0:T(8,128)S(1)} collective-permute-done((f32[128,128]{1,0:T(8,128)S(1)}, f32[128,128]{1,0:T(8,128)S(1)}, u32[]{:S(2)}, u32[]{:S(2)}) %collective-permute-start.2) | collective-permute-done | bytes 65568 | tf_op jit(solution)/shard_map/while/body/eval_jaxpr/ppermute | solution.py:12
  165.7 0.7 collective-permute-done.3
  169.4 3.1 %collective-permute-done = bf16[128,128]{1,0:T(8,128)(2,1)S(1)} collective-permute-done((bf16[128,128]{1,0:T(8,128)(2,1)S(1)}, bf16[128,128]{1,0:T(8,128)(2,1)S(1)}, u32[]{:S(2)}, u32[]{:S(2)}) %collective-permute-start) | collective-permute-done | bytes 32800 | tf_op jit(solution)/shard_map/while/body/eval_jaxpr/ppermute | solution.py:12
  172.8 2.4 %collective-permute-done.2 = f32[128,128]{1,0:T(8,128)S(1)} collective-permute-done((f32[128,128]{1,0:T(8,128)S(1)}, f32[128,128]{1,0:T(8,128)S(1)}, u32[]{:S(2)}, u32[]{:S(2)}) %collective-permute-start.2) | collective-permute-done | bytes 65568 | tf_op jit(solution)/shard_map/while/body/eval_jaxpr/ppermute | solution.py:12
  175.2 0.7 collective-permute-done.3
  178.9 3.1 %collective-permute-done = bf16[128,128]{1,0:T(8,128)(2,1)S(1)} collective-permute-done((bf16[128,128]{1,0:T(8,128)(2,1)S(1)}, bf16[128,128]{1,0:T(8,128)(2,1)S(1)}, u32[]{:S(2)}, u32[]{:S(2)}) %collective-permute-start) | collective-permute-done | bytes 32800 | tf_op jit(solution)/shard_map/while/body/eval_jaxpr/ppermute | solution.py:12
  182.3 2.4 %collective-permute-done.2 = f32[128,128]{1,0:T(8,128)S(1)} collective-permute-done((f32[128,128]{1,0:T(8,128)S(1)}, f32[128,128]{1,0:T(8,128)S(1)}, u32[]{:S(2)}, u32[]{:S(2)}) %collective-permute-start.2) | collective-permute-done | bytes 65568 | tf_op jit(solution)/shard_map/while/body/eval_jaxpr/ppermute | solution.py:12
  184.7 0.7 collective-permute-done.3
  188.4 3.1 %collective-permute-done = bf16[128,128]{1,0:T(8,128)(2,1)S(1)} collective-permute-done((bf16[128,128]{1,0:T(8,128)(2,1)S(1)}, bf16[128,128]{1,0:T(8,128)(2,1)S(1)}, u32[]{:S(2)}, u32[]{:S(2)}) %collective-permute-start) | collective-permute-done | bytes 32800 | tf_op jit(solution)/shard_map/while/body/eval_jaxpr/ppermute | solution.py:12
  191.8 2.4 %collective-permute-done.2 = f32[128,128]{1,0:T(8,128)S(1)} collective-permute-done((f32[128,128]{1,0:T(8,128)S(1)}, f32[128,128]{1,0:T(8,128)S(1)}, u32[]{:S(2)}, u32[]{:S(2)}) %collective-permute-start.2) | collective-permute-done | bytes 65568 | tf_op jit(solution)/shard_map/while/body/eval_jaxpr/ppermute | solution.py:12
  197.9 3.1 %collective-permute-done = bf16[128,128]{1,0:T(8,128)(2,1)S(1)} collective-permute-done((bf16[128,128]{1,0:T(8,128)(2,1)S(1)}, bf16[128,128]{1,0:T(8,128)(2,1)S(1)}, u32[]{:S(2)}, u32[]{:S(2)}) %collective-permute-start) | collective-permute-done | bytes 32800 | tf_op jit(solution)/shard_map/while/body/eval_jaxpr/ppermute | solution.py:12
  201.4 2.4 %collective-permute-done.2 = f32[128,128]{1,0:T(8,128)S(1)} collective-permute-done((f32[128,128]{1,0:T(8,128)S(1)}, f32[128,128]{1,0:T(8,128)S(1)}, u32[]{:S(2)}, u32[]{:S(2)}) %collective-permute-start.2) | collective-permute-done | bytes 65568 | tf_op jit(solution)/shard_map/while/body/eval_jaxpr/ppermute | solution.py:12
  207.5 3.1 %collective-permute-done = bf16[128,128]{1,0:T(8,128)(2,1)S(1)} collective-permute-done((bf16[128,128]{1,0:T(8,128)(2,1)S(1)}, bf16[128,128]{1,0:T(8,128)(2,1)S(1)}, u32[]{:S(2)}, u32[]{:S(2)}) %collective-permute-start) | collective-permute-done | bytes 32800 | tf_op jit(solution)/shard_map/while/body/eval_jaxpr/ppermute | solution.py:12
  210.9 2.4 %collective-permute-done.2 = f32[128,128]{1,0:T(8,128)S(1)} collective-permute-done((f32[128,128]{1,0:T(8,128)S(1)}, f32[128,128]{1,0:T(8,128)S(1)}, u32[]{:S(2)}, u32[]{:S(2)}) %collective-permute-start.2) | collective-permute-done | bytes 65568 | tf_op jit(solution)/shard_map/while/body/eval_jaxpr/ppermute | solution.py:12
  216.7 4.2 %collective-permute-done.5 = f32[128,128]{1,0:T(8,128)S(1)} collective-permute-done((f32[128,128]{1,0:T(8,128)S(1)}, f32[128,128]{1,0:T(8,128)S(1)}, u32[]{:S(2)}, u32[]{:S(2)}) %collective-permute-start.5) | collective-permute-done | bytes 65568 | tf_op jit(solution)/shard_map/ppermute | solution.py:12
  (505 shorter events, 66.0 us)
Async XLA Ops:
  69.3 6.1 %collective-permute-start = (bf16[128,128]{1,0:T(8,128)(2,1)S(1)}, bf16[128,128]{1,0:T(8,128)(2,1)S(1)}, u32[]{:S(2)}, u32[]{:S(2)}) collective-permute-start(bf16[128,128]{1,0:T(8,128)(2,1)S(1)} %copy.67), channel_id=1, source_target_pairs={{0,1},{1,2},{2,3},{3,4},{4,5},{5,6},{6,7},{7,8},{8,9},{9,10},{10,1... | collective-permute-start | bytes 98312 | tf_op jit(solution)/shard_map/while/body/eval_jaxpr/ppermute | solution.py:12
  73.4 6.4 %collective-permute-start.2 = (f32[128,128]{1,0:T(8,128)S(1)}, f32[128,128]{1,0:T(8,128)S(1)}, u32[]{:S(2)}, u32[]{:S(2)}) collective-permute-start(f32[128,128]{1,0:T(8,128)S(1)} %fusion.122), channel_id=1, source_target_pairs={{0,1},{1,2},{2,3},{3,4},{4,5},{5,6},{6,7},{7,8},{8,9},{9,10},{10,1... | collective-permute-start | bytes 196616 | tf_op jit(solution)/shard_map/while/body/eval_jaxpr/ppermute | solution.py:12
  74.1 6.5 %collective-permute-start.3 = (f32[128,128]{1,0:T(8,128)S(1)}, f32[128,128]{1,0:T(8,128)S(1)}, u32[]{:S(2)}, u32[]{:S(2)}) collective-permute-start(f32[128,128]{1,0:T(8,128)S(1)} %convolution_add_fusion.6), channel_id=1, source_target_pairs={{0,1},{1,2},{2,3},{3,4},{4,5},{5,6},{6,7},{7,8},{8,9},{9,10},{10,1... | collective-permute-start | bytes 196616 | tf_op jit(solution)/shard_map/while/body/eval_jaxpr/ppermute | solution.py:12
  80.6 6.4 %collective-permute-start.1 = (bf16[128,128]{1,0:T(8,128)(2,1)S(1)}, bf16[128,128]{1,0:T(8,128)(2,1)S(1)}, u32[]{:S(2)}, u32[]{:S(2)}) collective-permute-start(bf16[128,128]{1,0:T(8,128)(2,1)S(1)} %copy.68), channel_id=1, source_target_pairs={{0,1},{1,2},{2,3},{3,4},{4,5},{5,6},{6,7},{7,8},{8,9},{9,10},{10,1... | collective-permute-start | bytes 98312 | tf_op jit(solution)/shard_map/while/body/eval_jaxpr/ppermute | solution.py:12
  83.0 6.4 %collective-permute-start.2 = (f32[128,128]{1,0:T(8,128)S(1)}, f32[128,128]{1,0:T(8,128)S(1)}, u32[]{:S(2)}, u32[]{:S(2)}) collective-permute-start(f32[128,128]{1,0:T(8,128)S(1)} %fusion.122), channel_id=1, source_target_pairs={{0,1},{1,2},{2,3},{3,4},{4,5},{5,6},{6,7},{7,8},{8,9},{9,10},{10,1... | collective-permute-start | bytes 196616 | tf_op jit(solution)/shard_map/while/body/eval_jaxpr/ppermute | solution.py:12
  83.3 6.8 %collective-permute-start.3 = (f32[128,128]{1,0:T(8,128)S(1)}, f32[128,128]{1,0:T(8,128)S(1)}, u32[]{:S(2)}, u32[]{:S(2)}) collective-permute-start(f32[128,128]{1,0:T(8,128)S(1)} %convolution_add_fusion.6), channel_id=1, source_target_pairs={{0,1},{1,2},{2,3},{3,4},{4,5},{5,6},{6,7},{7,8},{8,9},{9,10},{10,1... | collective-permute-start | bytes 196616 | tf_op jit(solution)/shard_map/while/body/eval_jaxpr/ppermute | solution.py:12
  90.1 6.4 %collective-permute-start.1 = (bf16[128,128]{1,0:T(8,128)(2,1)S(1)}, bf16[128,128]{1,0:T(8,128)(2,1)S(1)}, u32[]{:S(2)}, u32[]{:S(2)}) collective-permute-start(bf16[128,128]{1,0:T(8,128)(2,1)S(1)} %copy.68), channel_id=1, source_target_pairs={{0,1},{1,2},{2,3},{3,4},{4,5},{5,6},{6,7},{7,8},{8,9},{9,10},{10,1... | collective-permute-start | bytes 98312 | tf_op jit(solution)/shard_map/while/body/eval_jaxpr/ppermute | solution.py:12
  92.5 6.4 %collective-permute-start.2 = (f32[128,128]{1,0:T(8,128)S(1)}, f32[128,128]{1,0:T(8,128)S(1)}, u32[]{:S(2)}, u32[]{:S(2)}) collective-permute-start(f32[128,128]{1,0:T(8,128)S(1)} %fusion.122), channel_id=1, source_target_pairs={{0,1},{1,2},{2,3},{3,4},{4,5},{5,6},{6,7},{7,8},{8,9},{9,10},{10,1... | collective-permute-start | bytes 196616 | tf_op jit(solution)/shard_map/while/body/eval_jaxpr/ppermute | solution.py:12
  92.8 6.8 %collective-permute-start.3 = (f32[128,128]{1,0:T(8,128)S(1)}, f32[128,128]{1,0:T(8,128)S(1)}, u32[]{:S(2)}, u32[]{:S(2)}) collective-permute-start(f32[128,128]{1,0:T(8,128)S(1)} %convolution_add_fusion.6), channel_id=1, source_target_pairs={{0,1},{1,2},{2,3},{3,4},{4,5},{5,6},{6,7},{7,8},{8,9},{9,10},{10,1... | collective-permute-start | bytes 196616 | tf_op jit(solution)/shard_map/while/body/eval_jaxpr/ppermute | solution.py:12
  99.6 6.0 %collective-permute-start = (bf16[128,128]{1,0:T(8,128)(2,1)S(1)}, bf16[128,128]{1,0:T(8,128)(2,1)S(1)}, u32[]{:S(2)}, u32[]{:S(2)}) collective-permute-start(bf16[128,128]{1,0:T(8,128)(2,1)S(1)} %copy.67), channel_id=1, source_target_pairs={{0,1},{1,2},{2,3},{3,4},{4,5},{5,6},{6,7},{7,8},{8,9},{9,10},{10,1... | collective-permute-start | bytes 98312 | tf_op jit(solution)/shard_map/while/body/eval_jaxpr/ppermute | solution.py:12
  99.7 6.4 %collective-permute-start.1 = (bf16[128,128]{1,0:T(8,128)(2,1)S(1)}, bf16[128,128]{1,0:T(8,128)(2,1)S(1)}, u32[]{:S(2)}, u32[]{:S(2)}) collective-permute-start(bf16[128,128]{1,0:T(8,128)(2,1)S(1)} %copy.68), channel_id=1, source_target_pairs={{0,1},{1,2},{2,3},{3,4},{4,5},{5,6},{6,7},{7,8},{8,9},{9,10},{10,1... | collective-permute-start | bytes 98312 | tf_op jit(solution)/shard_map/while/body/eval_jaxpr/ppermute | solution.py:12
  102.0 6.4 %collective-permute-start.2 = (f32[128,128]{1,0:T(8,128)S(1)}, f32[128,128]{1,0:T(8,128)S(1)}, u32[]{:S(2)}, u32[]{:S(2)}) collective-permute-start(f32[128,128]{1,0:T(8,128)S(1)} %fusion.122), channel_id=1, source_target_pairs={{0,1},{1,2},{2,3},{3,4},{4,5},{5,6},{6,7},{7,8},{8,9},{9,10},{10,1... | collective-permute-start | bytes 196616 | tf_op jit(solution)/shard_map/while/body/eval_jaxpr/ppermute | solution.py:12
  102.3 6.8 %collective-permute-start.3 = (f32[128,128]{1,0:T(8,128)S(1)}, f32[128,128]{1,0:T(8,128)S(1)}, u32[]{:S(2)}, u32[]{:S(2)}) collective-permute-start(f32[128,128]{1,0:T(8,128)S(1)} %convolution_add_fusion.6), channel_id=1, source_target_pairs={{0,1},{1,2},{2,3},{3,4},{4,5},{5,6},{6,7},{7,8},{8,9},{9,10},{10,1... | collective-permute-start | bytes 196616 | tf_op jit(solution)/shard_map/while/body/eval_jaxpr/ppermute | solution.py:12
  109.2 6.4 %collective-permute-start.1 = (bf16[128,128]{1,0:T(8,128)(2,1)S(1)}, bf16[128,128]{1,0:T(8,128)(2,1)S(1)}, u32[]{:S(2)}, u32[]{:S(2)}) collective-permute-start(bf16[128,128]{1,0:T(8,128)(2,1)S(1)} %copy.68), channel_id=1, source_target_pairs={{0,1},{1,2},{2,3},{3,4},{4,5},{5,6},{6,7},{7,8},{8,9},{9,10},{10,1... | collective-permute-start | bytes 98312 | tf_op jit(solution)/shard_map/while/body/eval_jaxpr/ppermute | solution.py:12
  111.6 6.4 %collective-permute-start.2 = (f32[128,128]{1,0:T(8,128)S(1)}, f32[128,128]{1,0:T(8,128)S(1)}, u32[]{:S(2)}, u32[]{:S(2)}) collective-permute-start(f32[128,128]{1,0:T(8,128)S(1)} %fusion.122), channel_id=1, source_target_pairs={{0,1},{1,2},{2,3},{3,4},{4,5},{5,6},{6,7},{7,8},{8,9},{9,10},{10,1... | collective-permute-start | bytes 196616 | tf_op jit(solution)/shard_map/while/body/eval_jaxpr/ppermute | solution.py:12
  111.9 6.8 %collective-permute-start.3 = (f32[128,128]{1,0:T(8,128)S(1)}, f32[128,128]{1,0:T(8,128)S(1)}, u32[]{:S(2)}, u32[]{:S(2)}) collective-permute-start(f32[128,128]{1,0:T(8,128)S(1)} %convolution_add_fusion.6), channel_id=1, source_target_pairs={{0,1},{1,2},{2,3},{3,4},{4,5},{5,6},{6,7},{7,8},{8,9},{9,10},{10,1... | collective-permute-start | bytes 196616 | tf_op jit(solution)/shard_map/while/body/eval_jaxpr/ppermute | solution.py:12
  118.7 6.4 %collective-permute-start.1 = (bf16[128,128]{1,0:T(8,128)(2,1)S(1)}, bf16[128,128]{1,0:T(8,128)(2,1)S(1)}, u32[]{:S(2)}, u32[]{:S(2)}) collective-permute-start(bf16[128,128]{1,0:T(8,128)(2,1)S(1)} %copy.68), channel_id=1, source_target_pairs={{0,1},{1,2},{2,3},{3,4},{4,5},{5,6},{6,7},{7,8},{8,9},{9,10},{10,1... | collective-permute-start | bytes 98312 | tf_op jit(solution)/shard_map/while/body/eval_jaxpr/ppermute | solution.py:12
  121.1 6.4 %collective-permute-start.2 = (f32[128,128]{1,0:T(8,128)S(1)}, f32[128,128]{1,0:T(8,128)S(1)}, u32[]{:S(2)}, u32[]{:S(2)}) collective-permute-start(f32[128,128]{1,0:T(8,128)S(1)} %fusion.122), channel_id=1, source_target_pairs={{0,1},{1,2},{2,3},{3,4},{4,5},{5,6},{6,7},{7,8},{8,9},{9,10},{10,1... | collective-permute-start | bytes 196616 | tf_op jit(solution)/shard_map/while/body/eval_jaxpr/ppermute | solution.py:12
  121.4 6.8 %collective-permute-start.3 = (f32[128,128]{1,0:T(8,128)S(1)}, f32[128,128]{1,0:T(8,128)S(1)}, u32[]{:S(2)}, u32[]{:S(2)}) collective-permute-start(f32[128,128]{1,0:T(8,128)S(1)} %convolution_add_fusion.6), channel_id=1, source_target_pairs={{0,1},{1,2},{2,3},{3,4},{4,5},{5,6},{6,7},{7,8},{8,9},{9,10},{10,1... | collective-permute-start | bytes 196616 | tf_op jit(solution)/shard_map/while/body/eval_jaxpr/ppermute | solution.py:12
  128.3 6.4 %collective-permute-start.1 = (bf16[128,128]{1,0:T(8,128)(2,1)S(1)}, bf16[128,128]{1,0:T(8,128)(2,1)S(1)}, u32[]{:S(2)}, u32[]{:S(2)}) collective-permute-start(bf16[128,128]{1,0:T(8,128)(2,1)S(1)} %copy.68), channel_id=1, source_target_pairs={{0,1},{1,2},{2,3},{3,4},{4,5},{5,6},{6,7},{7,8},{8,9},{9,10},{10,1... | collective-permute-start | bytes 98312 | tf_op jit(solution)/shard_map/while/body/eval_jaxpr/ppermute | solution.py:12
  130.6 6.4 %collective-permute-start.2 = (f32[128,128]{1,0:T(8,128)S(1)}, f32[128,128]{1,0:T(8,128)S(1)}, u32[]{:S(2)}, u32[]{:S(2)}) collective-permute-start(f32[128,128]{1,0:T(8,128)S(1)} %fusion.122), channel_id=1, source_target_pairs={{0,1},{1,2},{2,3},{3,4},{4,5},{5,6},{6,7},{7,8},{8,9},{9,10},{10,1... | collective-permute-start | bytes 196616 | tf_op jit(solution)/shard_map/while/body/eval_jaxpr/ppermute | solution.py:12
  130.9 6.8 %collective-permute-start.3 = (f32[128,128]{1,0:T(8,128)S(1)}, f32[128,128]{1,0:T(8,128)S(1)}, u32[]{:S(2)}, u32[]{:S(2)}) collective-permute-start(f32[128,128]{1,0:T(8,128)S(1)} %convolution_add_fusion.6), channel_id=1, source_target_pairs={{0,1},{1,2},{2,3},{3,4},{4,5},{5,6},{6,7},{7,8},{8,9},{9,10},{10,1... | collective-permute-start | bytes 196616 | tf_op jit(solution)/shard_map/while/body/eval_jaxpr/ppermute | solution.py:12
  137.8 6.4 %collective-permute-start.1 = (bf16[128,128]{1,0:T(8,128)(2,1)S(1)}, bf16[128,128]{1,0:T(8,128)(2,1)S(1)}, u32[]{:S(2)}, u32[]{:S(2)}) collective-permute-start(bf16[128,128]{1,0:T(8,128)(2,1)S(1)} %copy.68), channel_id=1, source_target_pairs={{0,1},{1,2},{2,3},{3,4},{4,5},{5,6},{6,7},{7,8},{8,9},{9,10},{10,1... | collective-permute-start | bytes 98312 | tf_op jit(solution)/shard_map/while/body/eval_jaxpr/ppermute | solution.py:12
  140.2 6.4 %collective-permute-start.2 = (f32[128,128]{1,0:T(8,128)S(1)}, f32[128,128]{1,0:T(8,128)S(1)}, u32[]{:S(2)}, u32[]{:S(2)}) collective-permute-start(f32[128,128]{1,0:T(8,128)S(1)} %fusion.122), channel_id=1, source_target_pairs={{0,1},{1,2},{2,3},{3,4},{4,5},{5,6},{6,7},{7,8},{8,9},{9,10},{10,1... | collective-permute-start | bytes 196616 | tf_op jit(solution)/shard_map/while/body/eval_jaxpr/ppermute | solution.py:12
  140.5 6.8 %collective-permute-start.3 = (f32[128,128]{1,0:T(8,128)S(1)}, f32[128,128]{1,0:T(8,128)S(1)}, u32[]{:S(2)}, u32[]{:S(2)}) collective-permute-start(f32[128,128]{1,0:T(8,128)S(1)} %convolution_add_fusion.6), channel_id=1, source_target_pairs={{0,1},{1,2},{2,3},{3,4},{4,5},{5,6},{6,7},{7,8},{8,9},{9,10},{10,1... | collective-permute-start | bytes 196616 | tf_op jit(solution)/shard_map/while/body/eval_jaxpr/ppermute | solution.py:12
  147.3 6.4 %collective-permute-start.1 = (bf16[128,128]{1,0:T(8,128)(2,1)S(1)}, bf16[128,128]{1,0:T(8,128)(2,1)S(1)}, u32[]{:S(2)}, u32[]{:S(2)}) collective-permute-start(bf16[128,128]{1,0:T(8,128)(2,1)S(1)} %copy.68), channel_id=1, source_target_pairs={{0,1},{1,2},{2,3},{3,4},{4,5},{5,6},{6,7},{7,8},{8,9},{9,10},{10,1... | collective-permute-start | bytes 98312 | tf_op jit(solution)/shard_map/while/body/eval_jaxpr/ppermute | solution.py:12
  149.7 6.4 %collective-permute-start.2 = (f32[128,128]{1,0:T(8,128)S(1)}, f32[128,128]{1,0:T(8,128)S(1)}, u32[]{:S(2)}, u32[]{:S(2)}) collective-permute-start(f32[128,128]{1,0:T(8,128)S(1)} %fusion.122), channel_id=1, source_target_pairs={{0,1},{1,2},{2,3},{3,4},{4,5},{5,6},{6,7},{7,8},{8,9},{9,10},{10,1... | collective-permute-start | bytes 196616 | tf_op jit(solution)/shard_map/while/body/eval_jaxpr/ppermute | solution.py:12
  150.0 6.8 %collective-permute-start.3 = (f32[128,128]{1,0:T(8,128)S(1)}, f32[128,128]{1,0:T(8,128)S(1)}, u32[]{:S(2)}, u32[]{:S(2)}) collective-permute-start(f32[128,128]{1,0:T(8,128)S(1)} %convolution_add_fusion.6), channel_id=1, source_target_pairs={{0,1},{1,2},{2,3},{3,4},{4,5},{5,6},{6,7},{7,8},{8,9},{9,10},{10,1... | collective-permute-start | bytes 196616 | tf_op jit(solution)/shard_map/while/body/eval_jaxpr/ppermute | solution.py:12
  156.9 6.4 %collective-permute-start.1 = (bf16[128,128]{1,0:T(8,128)(2,1)S(1)}, bf16[128,128]{1,0:T(8,128)(2,1)S(1)}, u32[]{:S(2)}, u32[]{:S(2)}) collective-permute-start(bf16[128,128]{1,0:T(8,128)(2,1)S(1)} %copy.68), channel_id=1, source_target_pairs={{0,1},{1,2},{2,3},{3,4},{4,5},{5,6},{6,7},{7,8},{8,9},{9,10},{10,1... | collective-permute-start | bytes 98312 | tf_op jit(solution)/shard_map/while/body/eval_jaxpr/ppermute | solution.py:12
  159.2 6.4 %collective-permute-start.2 = (f32[128,128]{1,0:T(8,128)S(1)}, f32[128,128]{1,0:T(8,128)S(1)}, u32[]{:S(2)}, u32[]{:S(2)}) collective-permute-start(f32[128,128]{1,0:T(8,128)S(1)} %fusion.122), channel_id=1, source_target_pairs={{0,1},{1,2},{2,3},{3,4},{4,5},{5,6},{6,7},{7,8},{8,9},{9,10},{10,1... | collective-permute-start | bytes 196616 | tf_op jit(solution)/shard_map/while/body/eval_jaxpr/ppermute | solution.py:12
  159.5 6.8 %collective-permute-start.3 = (f32[128,128]{1,0:T(8,128)S(1)}, f32[128,128]{1,0:T(8,128)S(1)}, u32[]{:S(2)}, u32[]{:S(2)}) collective-permute-start(f32[128,128]{1,0:T(8,128)S(1)} %convolution_add_fusion.6), channel_id=1, source_target_pairs={{0,1},{1,2},{2,3},{3,4},{4,5},{5,6},{6,7},{7,8},{8,9},{9,10},{10,1... | collective-permute-start | bytes 196616 | tf_op jit(solution)/shard_map/while/body/eval_jaxpr/ppermute | solution.py:12
  166.4 6.4 %collective-permute-start.1 = (bf16[128,128]{1,0:T(8,128)(2,1)S(1)}, bf16[128,128]{1,0:T(8,128)(2,1)S(1)}, u32[]{:S(2)}, u32[]{:S(2)}) collective-permute-start(bf16[128,128]{1,0:T(8,128)(2,1)S(1)} %copy.68), channel_id=1, source_target_pairs={{0,1},{1,2},{2,3},{3,4},{4,5},{5,6},{6,7},{7,8},{8,9},{9,10},{10,1... | collective-permute-start | bytes 98312 | tf_op jit(solution)/shard_map/while/body/eval_jaxpr/ppermute | solution.py:12
  168.8 6.4 %collective-permute-start.2 = (f32[128,128]{1,0:T(8,128)S(1)}, f32[128,128]{1,0:T(8,128)S(1)}, u32[]{:S(2)}, u32[]{:S(2)}) collective-permute-start(f32[128,128]{1,0:T(8,128)S(1)} %fusion.122), channel_id=1, source_target_pairs={{0,1},{1,2},{2,3},{3,4},{4,5},{5,6},{6,7},{7,8},{8,9},{9,10},{10,1... | collective-permute-start | bytes 196616 | tf_op jit(solution)/shard_map/while/body/eval_jaxpr/ppermute | solution.py:12
  169.1 6.8 %collective-permute-start.3 = (f32[128,128]{1,0:T(8,128)S(1)}, f32[128,128]{1,0:T(8,128)S(1)}, u32[]{:S(2)}, u32[]{:S(2)}) collective-permute-start(f32[128,128]{1,0:T(8,128)S(1)} %convolution_add_fusion.6), channel_id=1, source_target_pairs={{0,1},{1,2},{2,3},{3,4},{4,5},{5,6},{6,7},{7,8},{8,9},{9,10},{10,1... | collective-permute-start | bytes 196616 | tf_op jit(solution)/shard_map/while/body/eval_jaxpr/ppermute | solution.py:12
  175.9 6.4 %collective-permute-start.1 = (bf16[128,128]{1,0:T(8,128)(2,1)S(1)}, bf16[128,128]{1,0:T(8,128)(2,1)S(1)}, u32[]{:S(2)}, u32[]{:S(2)}) collective-permute-start(bf16[128,128]{1,0:T(8,128)(2,1)S(1)} %copy.68), channel_id=1, source_target_pairs={{0,1},{1,2},{2,3},{3,4},{4,5},{5,6},{6,7},{7,8},{8,9},{9,10},{10,1... | collective-permute-start | bytes 98312 | tf_op jit(solution)/shard_map/while/body/eval_jaxpr/ppermute | solution.py:12
  178.3 6.4 %collective-permute-start.2 = (f32[128,128]{1,0:T(8,128)S(1)}, f32[128,128]{1,0:T(8,128)S(1)}, u32[]{:S(2)}, u32[]{:S(2)}) collective-permute-start(f32[128,128]{1,0:T(8,128)S(1)} %fusion.122), channel_id=1, source_target_pairs={{0,1},{1,2},{2,3},{3,4},{4,5},{5,6},{6,7},{7,8},{8,9},{9,10},{10,1... | collective-permute-start | bytes 196616 | tf_op jit(solution)/shard_map/while/body/eval_jaxpr/ppermute | solution.py:12
  178.6 6.8 %collective-permute-start.3 = (f32[128,128]{1,0:T(8,128)S(1)}, f32[128,128]{1,0:T(8,128)S(1)}, u32[]{:S(2)}, u32[]{:S(2)}) collective-permute-start(f32[128,128]{1,0:T(8,128)S(1)} %convolution_add_fusion.6), channel_id=1, source_target_pairs={{0,1},{1,2},{2,3},{3,4},{4,5},{5,6},{6,7},{7,8},{8,9},{9,10},{10,1... | collective-permute-start | bytes 196616 | tf_op jit(solution)/shard_map/while/body/eval_jaxpr/ppermute | solution.py:12
  185.5 6.4 %collective-permute-start.1 = (bf16[128,128]{1,0:T(8,128)(2,1)S(1)}, bf16[128,128]{1,0:T(8,128)(2,1)S(1)}, u32[]{:S(2)}, u32[]{:S(2)}) collective-permute-start(bf16[128,128]{1,0:T(8,128)(2,1)S(1)} %copy.68), channel_id=1, source_target_pairs={{0,1},{1,2},{2,3},{3,4},{4,5},{5,6},{6,7},{7,8},{8,9},{9,10},{10,1... | collective-permute-start | bytes 98312 | tf_op jit(solution)/shard_map/while/body/eval_jaxpr/ppermute | solution.py:12
  187.8 6.4 %collective-permute-start.2 = (f32[128,128]{1,0:T(8,128)S(1)}, f32[128,128]{1,0:T(8,128)S(1)}, u32[]{:S(2)}, u32[]{:S(2)}) collective-permute-start(f32[128,128]{1,0:T(8,128)S(1)} %fusion.122), channel_id=1, source_target_pairs={{0,1},{1,2},{2,3},{3,4},{4,5},{5,6},{6,7},{7,8},{8,9},{9,10},{10,1... | collective-permute-start | bytes 196616 | tf_op jit(solution)/shard_map/while/body/eval_jaxpr/ppermute | solution.py:12
  188.1 6.8 %collective-permute-start.3 = (f32[128,128]{1,0:T(8,128)S(1)}, f32[128,128]{1,0:T(8,128)S(1)}, u32[]{:S(2)}, u32[]{:S(2)}) collective-permute-start(f32[128,128]{1,0:T(8,128)S(1)} %convolution_add_fusion.6), channel_id=1, source_target_pairs={{0,1},{1,2},{2,3},{3,4},{4,5},{5,6},{6,7},{7,8},{8,9},{9,10},{10,1... | collective-permute-start | bytes 196616 | tf_op jit(solution)/shard_map/while/body/eval_jaxpr/ppermute | solution.py:12
  195.0 6.4 %collective-permute-start.1 = (bf16[128,128]{1,0:T(8,128)(2,1)S(1)}, bf16[128,128]{1,0:T(8,128)(2,1)S(1)}, u32[]{:S(2)}, u32[]{:S(2)}) collective-permute-start(bf16[128,128]{1,0:T(8,128)(2,1)S(1)} %copy.68), channel_id=1, source_target_pairs={{0,1},{1,2},{2,3},{3,4},{4,5},{5,6},{6,7},{7,8},{8,9},{9,10},{10,1... | collective-permute-start | bytes 98312 | tf_op jit(solution)/shard_map/while/body/eval_jaxpr/ppermute | solution.py:12
  197.4 6.4 %collective-permute-start.2 = (f32[128,128]{1,0:T(8,128)S(1)}, f32[128,128]{1,0:T(8,128)S(1)}, u32[]{:S(2)}, u32[]{:S(2)}) collective-permute-start(f32[128,128]{1,0:T(8,128)S(1)} %fusion.122), channel_id=1, source_target_pairs={{0,1},{1,2},{2,3},{3,4},{4,5},{5,6},{6,7},{7,8},{8,9},{9,10},{10,1... | collective-permute-start | bytes 196616 | tf_op jit(solution)/shard_map/while/body/eval_jaxpr/ppermute | solution.py:12
  197.7 6.8 %collective-permute-start.3 = (f32[128,128]{1,0:T(8,128)S(1)}, f32[128,128]{1,0:T(8,128)S(1)}, u32[]{:S(2)}, u32[]{:S(2)}) collective-permute-start(f32[128,128]{1,0:T(8,128)S(1)} %convolution_add_fusion.6), channel_id=1, source_target_pairs={{0,1},{1,2},{2,3},{3,4},{4,5},{5,6},{6,7},{7,8},{8,9},{9,10},{10,1... | collective-permute-start | bytes 196616 | tf_op jit(solution)/shard_map/while/body/eval_jaxpr/ppermute | solution.py:12
  204.5 6.4 %collective-permute-start.1 = (bf16[128,128]{1,0:T(8,128)(2,1)S(1)}, bf16[128,128]{1,0:T(8,128)(2,1)S(1)}, u32[]{:S(2)}, u32[]{:S(2)}) collective-permute-start(bf16[128,128]{1,0:T(8,128)(2,1)S(1)} %copy.68), channel_id=1, source_target_pairs={{0,1},{1,2},{2,3},{3,4},{4,5},{5,6},{6,7},{7,8},{8,9},{9,10},{10,1... | collective-permute-start | bytes 98312 | tf_op jit(solution)/shard_map/while/body/eval_jaxpr/ppermute | solution.py:12
  206.9 6.4 %collective-permute-start.2 = (f32[128,128]{1,0:T(8,128)S(1)}, f32[128,128]{1,0:T(8,128)S(1)}, u32[]{:S(2)}, u32[]{:S(2)}) collective-permute-start(f32[128,128]{1,0:T(8,128)S(1)} %fusion.122), channel_id=1, source_target_pairs={{0,1},{1,2},{2,3},{3,4},{4,5},{5,6},{6,7},{7,8},{8,9},{9,10},{10,1... | collective-permute-start | bytes 196616 | tf_op jit(solution)/shard_map/while/body/eval_jaxpr/ppermute | solution.py:12
  207.2 6.8 %collective-permute-start.3 = (f32[128,128]{1,0:T(8,128)S(1)}, f32[128,128]{1,0:T(8,128)S(1)}, u32[]{:S(2)}, u32[]{:S(2)}) collective-permute-start(f32[128,128]{1,0:T(8,128)S(1)} %convolution_add_fusion.6), channel_id=1, source_target_pairs={{0,1},{1,2},{2,3},{3,4},{4,5},{5,6},{6,7},{7,8},{8,9},{9,10},{10,1... | collective-permute-start | bytes 196616 | tf_op jit(solution)/shard_map/while/body/eval_jaxpr/ppermute | solution.py:12
  214.5 6.4 %collective-permute-start.5 = (f32[128,128]{1,0:T(8,128)S(1)}, f32[128,128]{1,0:T(8,128)S(1)}, u32[]{:S(2)}, u32[]{:S(2)}) collective-permute-start(f32[128,128]{1,0:T(8,128)S(1)} %convolution_add_fusion.2), channel_id=1, source_target_pairs={{0,1},{1,2},{2,3},{3,4},{4,5},{5,6},{6,7},{7,8},{8,9},{9,10},{10,1... | collective-permute-start | bytes 196616 | tf_op jit(solution)/shard_map/ppermute | solution.py:12
  215.0 6.7 %collective-permute-start.4 = (f32[128,128]{1,0:T(8,128)S(1)}, f32[128,128]{1,0:T(8,128)S(1)}, u32[]{:S(2)}, u32[]{:S(2)}) collective-permute-start(f32[128,128]{1,0:T(8,128)S(1)} %fusion.45), channel_id=1, source_target_pairs={{0,1},{1,2},{2,3},{3,4},{4,5},{5,6},{6,7},{7,8},{8,9},{9,10},{10,1... | collective-permute-start | bytes 196616 | tf_op jit(solution)/shard_map/ppermute | solution.py:12
  (18 other events, 109.8 us)
where the time goes:
time: 223 us
  waiting for transfers between devices  103 us (46%)
  blocking collectives  43.4 us (19%)
  matrix products  31.7 us (14%)
  local copies, waits for them, and re-layouts  17 us (8%)
  loops' own time  13 us (6%)
  other arithmetic  5.81 us (3%)
  starting transfers between devices  5 us (2%)
  between operations  4.08 us (2%)
    ppermute x62, waiting for transfers between devices, passed_along(): return lax.ppermute(value, axis, pairs)  103 us
    all_gather x1, blocking collectives, shards(): key_piece = lax.all_gather(key_states, 'blk', axis=0, tiled=True)  24.6 us
    all_gather x1, blocking collectives, shards(): value_piece = lax.all_gather(value_states, 'blk', axis=0, tiled=True)  18.9 us
    another operation x1, loops' own time, shards(): carry_state = lax.fori_loop(0, cycle_size - 1, key_turn, carry_state)  11.7 us
    dynamic_slice x16, local copies, waits for them, and re-layouts, key_step(): key_pos = block_order[source] * tok_rows + offsets  9.38 us
    dot_general x32, matrix products, mask_for(): jnp.dot(tile_rows, one_hot.T, preferred_element_type=jnp.float32) > 0.5  6.53 us
    ppermute x62, starting transfers between devices, passed_along(): return lax.ppermute(value, axis, pairs)  5 us
    dot_general x16, matrix products, softmax_update(): jnp.dot(weights.astype(jnp.bfloat16), value_sub, preferred_element_type=j...  4.83 us
  transfers between devices with their start and end apart: 62, of which 62 were waited for; matrix products, arithmetic and copies ran while one was open for 14% of the time, Pallas kernels for 0%

commit v1 on v0

v1 whole, which is shorter than its diff:
```python
import functools
import math

import jax
import jax.numpy as jnp
from jax import lax
from jax.experimental import pallas as pl
from jax.experimental.pallas import tpu as pltpu
from jax.sharding import PartitionSpec as P

MESH = pl.DeviceIdType.MESH
F32 = jnp.float32
BF16 = jnp.bfloat16
MASKED = -1e30


def dot(a, b):
    return jnp.dot(a, b, preferred_element_type=F32)


def kernel(
    n, q_ref, k_ref, v_ref, g_ref, mask_ref, order_ref, att_ref, dq_ref, dk_ref, dv_ref,
    kv, qr, qt, gr, gt, prob, dprob, maxes, acc, send_a, recv_a, send_b, recv_b, send_c, recv_c,
    gz_s, gz_r, gy_s, gy_r, gc_s, gc_r, a_s, a_r, b_s, b_r, c_s, c_r,
):
    m = n // 4
    tok, hd = k_ref.shape
    heads = q_ref.shape[1] // hd
    rows = heads * tok
    scale = hd ** -0.5
    to_exp2 = scale * math.log2(math.e)

    me = lax.axis_index("blk")
    z, y, c = me // 4, (me // 2) % 2, me % 2

    def index(rz, ry, rc):
        zz = lax.rem(z + rz, m)
        yy = 1 - y if ry else y
        cc = 1 - c if rc else c
        return (zz * 2 + yy) * 2 + cc

    def remote(src, dst, s_sem, r_sem, target):
        return pltpu.make_async_remote_copy(
            src_ref=src, dst_ref=dst, send_sem=s_sem, recv_sem=r_sem,
            device_id={"blk": target}, device_id_type=MESH,
        )

    partner, sibling = index(0, 1, 0), index(0, 0, 1)

    def gather_z(g):
        return remote(kv.at[0, 0, 0], kv.at[m - g, 0, 0], gz_s.at[g], gz_r.at[m - g], index(g, 0, 0))

    def gather_y(rz):
        return remote(kv.at[rz, 0, 0], kv.at[rz, 0, 1], gy_s.at[rz], gy_r.at[rz], partner)

    def gather_c(rz, ry):
        return remote(kv.at[rz, 0, ry], kv.at[rz, 1, ry], gc_s.at[rz, ry], gc_r.at[rz, ry], sibling)

    def sum_a(rz):
        return remote(send_a.at[rz], recv_a.at[rz], a_s.at[rz], a_r.at[rz], sibling)

    def sum_b(rz):
        return remote(send_b.at[rz], recv_b.at[rz], b_s.at[rz], b_r.at[rz], partner)

    def sum_c(rz):
        return remote(send_c.at[rz], recv_c.at[rz], c_s.at[rz], c_r.at[rz], index(rz, 0, 0))

    barrier = pltpu.get_barrier_semaphore()
    for other in [index(g, 0, 0) for g in range(1, m)] + [partner, sibling]:
        pl.semaphore_signal(barrier, inc=1, device_id={"blk": other}, device_id_type=MESH)
    kv[0, 0, 0, 0] = k_ref[...]
    kv[0, 0, 0, 1] = v_ref[...]
    pl.semaphore_wait(barrier, m + 1)

    order = sorted(range(1, m), key=lambda r: min(r, m - r))
    gather_y(0).start()
    gather_c(0, 0).start()
    for rz in order:
        gather_z(m - rz).start()

    for h in range(heads):
        cols = slice(h * hd, (h + 1) * hd)
        lanes = slice(h * tok, (h + 1) * tok)
        qr[lanes, :] = q_ref[:, cols]
        gr[lanes, :] = g_ref[:, cols]
        qt[:, lanes] = q_ref[:, cols].T
        gt[:, lanes] = g_ref[:, cols].T

    my_block = order_ref[me]
    key_ids = lax.broadcasted_iota(jnp.int32, (tok, rows), 0)
    row_ids = lax.broadcasted_iota(jnp.int32, (tok, rows), 1) % tok
    causal = jnp.where(row_ids >= key_ids, 0.0, MASKED).astype(F32)

    def bias(rz, rc, ry):
        if rz == 0 and rc == 0 and ry == 0:
            return causal
        block = order_ref[index(rz, ry, rc)]
        seen = (my_block > block) & (mask_ref[my_block, block] == 1)
        return jnp.where(seen, 0.0, MASKED).astype(F32)

    run_max = jnp.full((1, rows), MASKED, F32)
    run_sum = jnp.zeros((1, rows), F32)
    run_out = jnp.zeros((hd, rows), F32)
    parts = [(rc, ry) for rc in range(2) for ry in range(2)]

    def pump_y(rz):
        gather_y(rz).wait_recv()
        gather_c(rz, 1).start()

    def pump_z(rz):
        gather_z(m - rz).wait_recv()
        gather_y(rz).start()
        gather_c(rz, 0).start()

    steps = [0] + order
    pump_y(0)
    for step, rz in enumerate(steps):
        if step + 1 < len(steps):
            pump_z(steps[step + 1])
        gather_c(rz, 0).wait_recv()
        gather_c(rz, 1).wait_recv()
        keys = kv[rz, :, :, 0].reshape(4 * tok, hd)
        values = kv[rz, :, :, 1].reshape(4 * tok, hd)
        scores = dot(keys, qt[...])
        scores = [
            scores[i * tok:(i + 1) * tok] * to_exp2 + bias(rz, rc, ry)
            for i, (rc, ry) in enumerate(parts)
        ]
        dprob[rz] = dot(values, gt[...])
        new_max = run_max
        for s in scores:
            new_max = jnp.maximum(new_max, jnp.max(s, axis=0, keepdims=True))
        factor = jnp.exp2(run_max - new_max)
        run_sum = run_sum * factor
        for i, s in enumerate(scores):
            p = jnp.exp2(s - new_max)
            run_sum = run_sum + jnp.sum(p, axis=0, keepdims=True)
            prob[rz, i * tok:(i + 1) * tok, :] = p.astype(BF16)
        run_out = run_out * factor + dot(values.T, prob[rz])
        run_max = new_max
        maxes[rz] = new_max
        if step + 1 < len(steps):
            pump_y(steps[step + 1])

    inverse = 1.0 / run_sum
    out_t = (run_out * inverse).astype(BF16)
    delta = jnp.sum(gt[...].astype(F32) * out_t.astype(F32), axis=0, keepdims=True)

    def grads(rz):
        factor = jnp.exp2(maxes[rz] - run_max) * inverse
        wide, scored = [], []
        for i in range(4):
            part = slice(i * tok, (i + 1) * tok)
            w = prob[rz, part, :].astype(F32) * factor
            wide.append(w.astype(BF16))
            ds = (w * (dprob[rz, part, :] - delta)).astype(BF16)
            prob[rz, part, :] = ds
            scored.append(ds)
        dv = dot(jnp.concatenate(wide, axis=0), gr[...])
        dk = dot(jnp.concatenate(scored, axis=0), qr[...])
        for i, (rc, ry) in enumerate(parts):
            part = slice(i * tok, (i + 1) * tok)
            if rc:
                send_a[rz, ry, 0] = dk[part].astype(BF16)
                send_a[rz, ry, 1] = dv[part].astype(BF16)
            else:
                acc[rz, ry, 0] = dk[part]
                acc[rz, ry, 1] = dv[part]
        sum_a(rz).start()

    def level_b(rz):
        sum_a(rz).wait_recv()
        send_b[rz] = (acc[rz, 1] + recv_a[rz, 1].astype(F32)).astype(BF16)
        sum_b(rz).start()

    def level_c(rz):
        sum_b(rz).wait_recv()
        total = acc[rz, 0] + recv_a[rz, 0].astype(F32) + recv_b[rz].astype(F32)
        if rz == 0:
            acc[0, 0] = total
        else:
            send_c[rz] = total.astype(BF16)
            sum_c(rz).start()

    back = order[::-1] + [0]
    for step in range(m + 2):
        if step < m:
            grads(back[step])
        if 1 <= step <= m:
            level_b(back[step - 1])
        if 2 <= step:
            level_c(back[step - 2])

    dq_t = jnp.zeros((hd, rows), F32)
    for rz in range(m):
        dq_t = dq_t + dot(kv[rz, :, :, 0].reshape(4 * tok, hd).T, prob[rz])
    dq_t = (dq_t * scale).astype(BF16)
    for h in range(heads):
        cols = slice(h * hd, (h + 1) * hd)
        lanes = slice(h * tok, (h + 1) * tok)
        att_ref[:, cols] = out_t[:, lanes].T
        dq_ref[:, cols] = dq_t[:, lanes].T

    dk, dv = acc[0, 0, 0], acc[0, 0, 1]
    for rz in back[:-1]:
        sum_c(rz).wait_recv()
        dk = dk + recv_c[rz, 0].astype(F32)
        dv = dv + recv_c[rz, 1].astype(F32)
    dk_ref[...] = dk * scale
    dv_ref[...] = dv

    for rz in range(m):
        gather_y(rz).wait_send()
        gather_c(rz, 0).wait_send()
        gather_c(rz, 1).wait_send()
        sum_a(rz).wait_send()
        sum_b(rz).wait_send()
        if rz:
            gather_z(rz).wait_send()
            sum_c(rz).wait_send()


def shards(queries, key_states, value_states, grad_out, tile_mask, block_order):
    n = lax.axis_size("blk")
    m = n // 4
    tok, hd = key_states.shape
    rows = queries.shape[1] // hd * tok
    assert n == 4 * m and tile_mask.shape[1] == n
    vmem = pl.BlockSpec(memory_space=pltpu.VMEM)
    smem = pl.BlockSpec(memory_space=pltpu.SMEM)
    dma = pltpu.SemaphoreType.DMA
    return pl.pallas_call(
        functools.partial(kernel, n),
        out_shape=(
            jax.ShapeDtypeStruct(queries.shape, BF16),
            jax.ShapeDtypeStruct(queries.shape, BF16),
            jax.ShapeDtypeStruct(key_states.shape, F32),
            jax.ShapeDtypeStruct(key_states.shape, F32),
        ),
        in_specs=[vmem] * 4 + [smem] * 2,
        out_specs=(vmem,) * 4,
        scratch_shapes=[
            pltpu.VMEM((m, 2, 2, 2, tok, hd), BF16),
            pltpu.VMEM((rows, hd), BF16),
            pltpu.VMEM((hd, rows), BF16),
            pltpu.VMEM((rows, hd), BF16),
            pltpu.VMEM((hd, rows), BF16),
            pltpu.VMEM((m, 4 * tok, rows), BF16),
            pltpu.VMEM((m, 4 * tok, rows), F32),
            pltpu.VMEM((m, 1, rows), F32),
            pltpu.VMEM((m, 2, 2, tok, hd), F32),
            pltpu.VMEM((m, 2, 2, tok, hd), BF16),
            pltpu.VMEM((m, 2, 2, tok, hd), BF16),
            pltpu.VMEM((m, 2, tok, hd), BF16),
            pltpu.VMEM((m, 2, tok, hd), BF16),
            pltpu.VMEM((m, 2, tok, hd), BF16),
            pltpu.VMEM((m, 2, tok, hd), BF16),
            dma((m,)), dma((m,)), dma((m,)), dma((m,)), dma((m, 2)), dma((m, 2)),
            dma((m,)), dma((m,)), dma((m,)), dma((m,)), dma((m,)), dma((m,)),
        ],
        compiler_params=pltpu.CompilerParams(
            collective_id=0, has_side_effects=True, vmem_limit_bytes=56 * 1024 * 1024
        ),
    )(queries, key_states, value_states, grad_out, tile_mask, block_order)


def solution(mesh):
    both = P(("groups", "blk"), None)
    return jax.shard_map(
        shards,
        mesh=mesh,
        in_specs=(both, both, both, both, P("groups", None), P("groups")),
        out_specs=(both, both, both, both),
        check_vma=False,
    )
```

time: 223 us -> 42.4 us (0.19)
  waiting for transfers between devices: 103 us -> 0 us
  blocking collectives: 43.4 us -> 0 us
  Pallas kernels: 0 us -> 37.6 us
  matrix products: 31.7 us -> 0 us
  local copies, waits for them, and re-layouts: 17 us -> 3.96 us
  loops' own time: 13 us -> 0 us
  other arithmetic: 5.81 us -> 0 us
  starting transfers between devices: 5 us -> 0 us
  between operations: 4.08 us -> 0.65 us
    ppermute x62 -> x0, waiting for transfers between devices: 103 us -> none  [passed_along(): return lax.ppermute(value, axis, pairs)]
    all_gather x2 -> x0, blocking collectives: 43.4 us -> none  [the longest x1 24.6 us: shards(): key_piece = lax.all_gather(key_states, 'blk', axis=0, tiled=True)]
    pallas_call x0 -> x1, Pallas kernels: none -> 37.6 us  [shards(): pl.pallas_call(functools.partial(kernel, n), out_shape=(jax.ShapeDtypeStr...]
    dot_general x144 -> x0, matrix products: 31.7 us -> none  [the longest x32 6.53 us: mask_for(): jnp.dot(tile_rows, one_hot.T, preferred_element_type=jnp.float32) > 0.5]
    another operation x2 -> x0, loops' own time: 13 us -> none  [the longest x1 11.7 us: shards(): carry_state = lax.fori_loop(0, cycle_size - 1, key_turn, carry_state)]
    dynamic_slice x16 -> x0, local copies, waits for them, and re-layouts: 9.38 us -> none  [key_step(): key_pos = block_order[source] * tok_rows + offsets]
    ppermute x62 -> x0, starting transfers between devices: 5 us -> none  [passed_along(): return lax.ppermute(value, axis, pairs)]
    reduce_sum x33 -> x0, other arithmetic: 3.04 us -> none  [the longest x16 1.4 us: sub_step(): jnp.sum(jnp.where(owners[:, None] == jnp.arange(cycle_size, dtype=jnp.int...]
  transfers between devices with their start and end apart: 62 -> 0, of which waited for: 62 -> 0; matrix products, arithmetic and copies ran while one was open for 14% -> 0% of each run, Pallas kernels for 0% -> 0%
where the time goes in v1:
time: 42.4 us; the launch traced here: 42.2 us
  Pallas kernels  37.6 us (89%)
  local copies, waits for them, and re-layouts  3.96 us (9%)
  between operations  0.65 us (2%)
    pallas_call x1, Pallas kernels, shards(): pl.pallas_call(functools.partial(kernel, n), out_shape=(jax.ShapeDtypeStr...  37.6 us
    unnamed x10, local copies, waits for them, and re-layouts  3.96 us

profile of v1, /device:TPU:0, one launch (start us, length us, event | category | flops | bytes accessed | tf_op | source)
XLA Modules:
  0.0 42.2 jit_solution(7350167466791813852)
XLA Ops:
  0.6 37.6 %shard_map.93 = (bf16[128,512]{1,0:T(8,128)(2,1)}, bf16[128,512]{1,0:T(8,128)(2,1)}, f32[128,128]{1,0:T(8,128)}, f32[128,128]{1,0:T(8,128)}) custom-call(bf16[128,512]{1,0:T(8,128)(2,1)} %q_ref.1, bf16[128,128]{1,0:T(8,128)(2,1)} %k_ref.1, bf16[128,128]{1,0:T(8,128)(2,1)} %v_ref.1, bf16[128,512]{1,0:T(8,128)(2,1)} %g_ref.1, s32[16,16]{1,0:T(8,128)} %mask_ref.1, ...), custom_call_target="tpu_custom_call" | custom-call | tf_op jit(solution)/shard_map/pallas_call | solution.py:232
  38.2 0.0 copy-start
  38.2 1.6 %copy.14 = bf16[128,512]{1,0:T(8,128)(2,1)} copy(bf16[128,512]{1,0:T(8,128)(2,1)} %get-tuple-element.8) | data formatting | bytes 262144
  39.8 0.0 copy-done
  39.8 0.0 copy-start.2
  39.8 0.7 %copy.15 = bf16[128,512]{1,0:T(8,128)(2,1)} copy(bf16[128,512]{1,0:T(8,128)(2,1)S(1)} %copy-done) | data formatting | bytes 262144
  40.5 0.2 copy-done.2
  40.7 0.0 copy-start.1
  40.7 0.6 %copy.16 = f32[128,128]{1,0:T(8,128)} copy(f32[128,128]{1,0:T(8,128)S(1)} %copy-done.2) | data formatting | bytes 131072
  41.3 0.2 copy-done.1
  41.6 0.6 %copy.17 = f32[128,128]{1,0:T(8,128)} copy(f32[128,128]{1,0:T(8,128)S(1)} %copy-done.1) | data formatting | bytes 131072
Async XLA Ops:
  38.2 1.6 %copy-start = (bf16[128,512]{1,0:T(8,128)(2,1)S(1)}, bf16[128,512]{1,0:T(8,128)(2,1)}, u32[]{:S(2)}) copy-start(bf16[128,512]{1,0:T(8,128)(2,1)} %get-tuple-element.9) | copy-start | bytes 393220
  39.8 0.9 %copy-start.2 = (f32[128,128]{1,0:T(8,128)S(1)}, f32[128,128]{1,0:T(8,128)}, u32[]{:S(2)}) copy-start(f32[128,128]{1,0:T(8,128)} %get-tuple-element.10) | copy-start | bytes 196612
  40.7 0.9 %copy-start.1 = (f32[128,128]{1,0:T(8,128)S(1)}, f32[128,128]{1,0:T(8,128)}, u32[]{:S(2)}) copy-start(f32[128,128]{1,0:T(8,128)} %get-tuple-element.11) | copy-start | bytes 196612

commit v2 on v1

v2 whole, which is shorter than its diff:
```python
import functools
import math

import jax
import jax.numpy as jnp
from jax import lax
from jax.experimental import pallas as pl
from jax.experimental.pallas import tpu as pltpu
from jax.sharding import PartitionSpec as P

MESH = pl.DeviceIdType.MESH
F32 = jnp.float32
BF16 = jnp.bfloat16
MASKED = -1e30
VMEM_BYTES = 58 * 1024 * 1024


def dot(a, b):
    return jnp.dot(a, b, preferred_element_type=F32)


def kernel(
    n, q_hbm, k_hbm, v_hbm, g_hbm, mask_ref, order_ref, att_ref, dq_ref, dk_ref, dv_ref,
    q_ref, g_ref, kv, qr, qt, gr, gt, prob, dprob, maxes, acc, send_a, recv_a, send_b, recv_b, send_c, recv_c,
    in_s, gz_s, gz_r, gy_s, gy_r, gc_s, gc_r, a_s, a_r, b_s, b_r, c_s, c_r,
):
    m = n // 4
    tok, hd = k_hbm.shape
    heads = q_hbm.shape[1] // hd
    rows = heads * tok
    scale = hd ** -0.5
    to_exp2 = scale * math.log2(math.e)
    KEY, VALUE = 0, 1

    me = lax.axis_index("blk")
    z, y, c = me // 4, (me // 2) % 2, me % 2

    def index(rz, ry, rc):
        zz = lax.rem(z + rz, m)
        yy = 1 - y if ry else y
        cc = 1 - c if rc else c
        return (zz * 2 + yy) * 2 + cc

    def remote(src, dst, s_sem, r_sem, target):
        return pltpu.make_async_remote_copy(
            src_ref=src, dst_ref=dst, send_sem=s_sem, recv_sem=r_sem,
            device_id={"blk": target}, device_id_type=MESH,
        )

    partner, sibling = index(0, 1, 1), index(0, 0, 1)

    def side(rz, ry):
        return (1 if rz else 0) ^ ry

    def gather_z(t, g):
        return remote(
            kv.at[t, 0, 0, 0], kv.at[t, m - g, 1, 0], gz_s.at[t, g], gz_r.at[t, m - g], index(g, 0, 1)
        )

    def gather_y(t, rz):
        return remote(
            kv.at[t, rz, side(rz, 0), 0], kv.at[t, rz, side(rz, 1), 1], gy_s.at[t, rz], gy_r.at[t, rz], partner
        )

    def gather_c(t, rz, ry):
        near = side(rz, ry)
        return remote(
            kv.at[t, rz, near, ry], kv.at[t, rz, 1 - near, ry], gc_s.at[t, rz, ry], gc_r.at[t, rz, ry], sibling
        )

    def sum_a(t, rz):
        return remote(send_a.at[t, rz], recv_a.at[t, rz], a_s.at[t, rz], a_r.at[t, rz], sibling)

    def sum_b(t, rz):
        return remote(send_b.at[t, rz], recv_b.at[t, rz], b_s.at[t, rz], b_r.at[t, rz], partner)

    def sum_c(t, rz):
        return remote(send_c.at[t, rz], recv_c.at[t, rz], c_s.at[t, rz], c_r.at[t, rz], index(rz, 0, 1))

    barrier = pltpu.get_barrier_semaphore()
    for other in [index(g, 0, 1) for g in range(1, m)] + [partner, sibling]:
        pl.semaphore_signal(barrier, inc=1, device_id={"blk": other}, device_id_type=MESH)
    loads = [
        pltpu.make_async_copy(src, dst, in_s.at[i])
        for i, (src, dst) in enumerate(
            [(k_hbm, kv.at[KEY, 0, 0, 0]), (v_hbm, kv.at[VALUE, 0, 0, 0]), (q_hbm, q_ref), (g_hbm, g_ref)]
        )
    ]
    for load in loads:
        load.start()
    for load in loads:
        load.wait()
    pl.semaphore_wait(barrier, m + 1)

    order = sorted(range(1, m), key=lambda r: min(r, m - r))
    steps = [0] + order
    back = order[::-1] + [0]
    for t in (KEY, VALUE):
        gather_y(t, 0).start()
        for rz in order:
            gather_z(t, m - rz).start()
        gather_c(t, 0, 0).start()

    for h in range(heads):
        cols = slice(h * hd, (h + 1) * hd)
        lanes = slice(h * tok, (h + 1) * tok)
        qr[lanes, :] = q_ref[:, cols]
        gr[lanes, :] = g_ref[:, cols]
        qt[:, lanes] = q_ref[:, cols].T
        gt[:, lanes] = g_ref[:, cols].T

    my_block = order_ref[me]
    key_ids = lax.broadcasted_iota(jnp.int32, (tok, rows), 0)
    row_ids = lax.broadcasted_iota(jnp.int32, (tok, rows), 1) % tok
    causal = jnp.where(row_ids >= key_ids, 0.0, MASKED).astype(F32)

    def bias(rz, rc, ry):
        if rz == 0 and rc == 0 and ry == 0:
            return causal
        block = order_ref[index(rz, ry, rc)]
        seen = (my_block > block) & (mask_ref[my_block, block] == 1)
        return jnp.where(seen, 0.0, MASKED).astype(F32)

    parts = [(rc, ry) for rc in range(2) for ry in range(2)]

    def pump_y(t, rz):
        gather_y(t, rz).wait_recv()
        gather_c(t, rz, 1).start()

    def pump_z(t, rz):
        gather_z(t, m - rz).wait_recv()
        gather_y(t, rz).start()
        gather_c(t, rz, 0).start()

    def landed(t, rz):
        gather_c(t, rz, 0).wait_recv()
        gather_c(t, rz, 1).wait_recv()
        return kv[t, rz].reshape(4 * tok, hd)

    def score(rz, run_max, run_sum):
        scores = dot(landed(KEY, rz), qt[...])
        scores = [
            scores[i * tok:(i + 1) * tok] * to_exp2 + bias(rz, rc, ry)
            for i, (rc, ry) in enumerate(parts)
        ]
        new_max = run_max
        for s in scores:
            new_max = jnp.maximum(new_max, jnp.max(s, axis=0, keepdims=True))
        run_sum = run_sum * jnp.exp2(run_max - new_max)
        for i, s in enumerate(scores):
            p = jnp.exp2(s - new_max)
            run_sum = run_sum + jnp.sum(p, axis=0, keepdims=True)
            prob[rz, i * tok:(i + 1) * tok, :] = p.astype(BF16)
        maxes[rz] = new_max
        return new_max, run_sum

    for rz in order:
        pump_z(KEY, rz)
    pump_y(KEY, 0)
    run_max = jnp.full((1, rows), MASKED, F32)
    run_sum = jnp.zeros((1, rows), F32)
    run_max, run_sum = score(0, run_max, run_sum)
    for rz in order:
        pump_y(KEY, rz)
        pump_z(VALUE, rz)
    pump_y(VALUE, 0)
    for rz in order:
        run_max, run_sum = score(rz, run_max, run_sum)
    inverse = 1.0 / run_sum

    def hand_over(t, rz, grad):
        for i, (rc, ry) in enumerate(parts):
            part = slice(i * tok, (i + 1) * tok)
            if rc != side(rz, ry):
                send_a[t, rz, ry] = grad[part].astype(BF16)
            else:
                acc[t, rz, ry] = grad[part]
        sum_a(t, rz).start()

    def value_grad(rz):
        factor = jnp.exp2(maxes[rz] - run_max) * inverse
        for i in range(4):
            part = slice(i * tok, (i + 1) * tok)
            prob[rz, part, :] = (prob[rz, part, :].astype(F32) * factor).astype(BF16)
        hand_over(VALUE, rz, dot(prob[rz], gr[...]))

    def key_grad(rz, delta):
        for i in range(4):
            part = slice(i * tok, (i + 1) * tok)
            ds = prob[rz, part, :].astype(F32) * (dprob[rz, part, :] - delta)
            prob[rz, part, :] = ds.astype(BF16)
        hand_over(KEY, rz, dot(prob[rz], qr[...]))

    def level_b(t, rz):
        sum_a(t, rz).wait_recv()
        send_b[t, rz] = (acc[t, rz, 1] + recv_a[t, rz, 1].astype(F32)).astype(BF16)
        sum_b(t, rz).start()

    def level_c(t, rz):
        sum_b(t, rz).wait_recv()
        total = acc[t, rz, 0] + recv_a[t, rz, 0].astype(F32) + recv_b[t, rz].astype(F32)
        if rz == 0:
            acc[t, 0, 0] = total
        else:
            send_c[t, rz] = total.astype(BF16)
            sum_c(t, rz).start()

    for step in range(m + 1):
        if step < m:
            value_grad(back[step])
        if step:
            level_b(VALUE, back[step - 1])
    for rz in order:
        pump_y(VALUE, rz)
    out_t = jnp.zeros((hd, rows), F32)
    for step, rz in enumerate(steps):
        values = landed(VALUE, rz)
        dprob[rz] = dot(values, gt[...])
        out_t = out_t + dot(values.T, prob[rz])
        level_c(VALUE, back[step])
    out_t = out_t.astype(BF16)
    delta = jnp.sum(gt[...].astype(F32) * out_t.astype(F32), axis=0, keepdims=True)

    for step in range(m + 1):
        if step < m:
            key_grad(back[step], delta)
        if step:
            level_b(KEY, back[step - 1])

    for rz in back:
        level_c(KEY, rz)

    dq_t = jnp.zeros((hd, rows), F32)
    for rz in range(m):
        dq_t = dq_t + dot(kv[KEY, rz].reshape(4 * tok, hd).T, prob[rz])
    dq_t = (dq_t * scale).astype(BF16)
    for h in range(heads):
        cols = slice(h * hd, (h + 1) * hd)
        lanes = slice(h * tok, (h + 1) * tok)
        att_ref[:, cols] = out_t[:, lanes].T
        dq_ref[:, cols] = dq_t[:, lanes].T

    for t, out_ref, by in ((VALUE, dv_ref, 1.0), (KEY, dk_ref, scale)):
        total = acc[t, 0, 0]
        for rz in back[:-1]:
            sum_c(t, rz).wait_recv()
            total = total + recv_c[t, rz].astype(F32)
        out_ref[...] = total * by

    for t in (KEY, VALUE):
        for rz in range(m):
            gather_y(t, rz).wait_send()
            gather_c(t, rz, 0).wait_send()
            gather_c(t, rz, 1).wait_send()
            sum_a(t, rz).wait_send()
            sum_b(t, rz).wait_send()
            if rz:
                gather_z(t, rz).wait_send()
                sum_c(t, rz).wait_send()


def write_out(*refs):
    ins, outs, held, in_s, out_s = refs[:4], refs[4:8], refs[8:12], refs[12], refs[13]
    loads = [pltpu.make_async_copy(ins[i], held[i], in_s.at[i]) for i in range(4)]
    stores = [pltpu.make_async_copy(held[i], outs[i], out_s.at[i]) for i in range(4)]
    for load in loads:
        load.start()
    for load, store in zip(loads, stores):
        load.wait()
        store.start()
    for store in stores:
        store.wait()


def shards(queries, key_states, value_states, grad_out, tile_mask, block_order):
    n = lax.axis_size("blk")
    m = n // 4
    tok, hd = key_states.shape
    rows = queries.shape[1] // hd * tok
    assert n == 4 * m and tile_mask.shape[1] == n
    hbm = pl.BlockSpec(memory_space=pl.ANY)
    vmem = pl.BlockSpec(memory_space=pltpu.VMEM)
    smem = pl.BlockSpec(memory_space=pltpu.SMEM)
    dma = pltpu.SemaphoreType.DMA
    shapes = (
        jax.ShapeDtypeStruct(queries.shape, BF16),
        jax.ShapeDtypeStruct(queries.shape, BF16),
        jax.ShapeDtypeStruct(key_states.shape, F32),
        jax.ShapeDtypeStruct(key_states.shape, F32),
    )
    results = pl.pallas_call(
        functools.partial(kernel, n),
        out_shape=shapes,
        in_specs=[hbm] * 4 + [smem] * 2,
        out_specs=(vmem,) * 4,
        scratch_shapes=[
            pltpu.VMEM(queries.shape, BF16),
            pltpu.VMEM(queries.shape, BF16),
            pltpu.VMEM((2, m, 2, 2, tok, hd), BF16),
            pltpu.VMEM((rows, hd), BF16),
            pltpu.VMEM((hd, rows), BF16),
            pltpu.VMEM((rows, hd), BF16),
            pltpu.VMEM((hd, rows), BF16),
            pltpu.VMEM((m, 4 * tok, rows), BF16),
            pltpu.VMEM((m, 4 * tok, rows), F32),
            pltpu.VMEM((m, 1, rows), F32),
            pltpu.VMEM((2, m, 2, tok, hd), F32),
            pltpu.VMEM((2, m, 2, tok, hd), BF16),
            pltpu.VMEM((2, m, 2, tok, hd), BF16),
            pltpu.VMEM((2, m, tok, hd), BF16),
            pltpu.VMEM((2, m, tok, hd), BF16),
            pltpu.VMEM((2, m, tok, hd), BF16),
            pltpu.VMEM((2, m, tok, hd), BF16),
            dma((4,)), dma((2, m)), dma((2, m)), dma((2, m)), dma((2, m)), dma((2, m, 2)), dma((2, m, 2)),
            dma((2, m)), dma((2, m)), dma((2, m)), dma((2, m)), dma((2, m)), dma((2, m)),
        ],
        compiler_params=pltpu.CompilerParams(
            collective_id=0, has_side_effects=True, vmem_limit_bytes=VMEM_BYTES
        ),
    )(queries, key_states, value_states, grad_out, tile_mask, block_order)
    return pl.pallas_call(
        write_out,
        out_shape=shapes,
        in_specs=[hbm] * 4,
        out_specs=(hbm,) * 4,
        scratch_shapes=[pltpu.VMEM(s.shape, s.dtype) for s in shapes] + [dma((4,)), dma((4,))],
        compiler_params=pltpu.CompilerParams(vmem_limit_bytes=VMEM_BYTES),
    )(*results)


def solution(mesh):
    both = P(("groups", "blk"), None)
    return jax.shard_map(
        shards,
        mesh=mesh,
        in_specs=(both, both, both, both, P("groups", None), P("groups")),
        out_specs=(both, both, both, both),
        check_vma=False,
    )
```

time: 42.4 us -> 35.1 us (0.83)
  local copies, waits for them, and re-layouts: 3.96 us -> 0 us
  Pallas kernels: 37.6 us -> 34.3 us
    unnamed x10 -> x0, local copies, waits for them, and re-layouts: 3.96 us -> none
    pallas_call x1 -> x2, Pallas kernels: 37.6 us -> 34.3 us  [the longest x1 32.5 us: shards(): pl.pallas_call(functools.partial(kernel, n), out_shape=shapes, in_specs=[...]
where the time goes in v2:
time: 35.1 us; the launch traced here: 34.9 us
  Pallas kernels  34.3 us (98%)
  between operations  0.64 us (2%)
    pallas_call x1, Pallas kernels, shards(): pl.pallas_call(functools.partial(kernel, n), out_shape=shapes, in_specs=[...  32.5 us
    pallas_call x1, Pallas kernels, shards(): pl.pallas_call(write_out, out_shape=shapes, in_specs=[hbm] * 4, out_specs...  1.73 us

profile of v2, /device:TPU:0, one launch (start us, length us, event | category | flops | bytes accessed | tf_op | source)
XLA Modules:
  0.0 34.9 jit_solution(15692101402460803109)
XLA Ops:
  0.6 32.5 %shard_map.93 = (bf16[128,512]{1,0:T(8,128)(2,1)}, bf16[128,512]{1,0:T(8,128)(2,1)}, f32[128,128]{1,0:T(8,128)}, f32[128,128]{1,0:T(8,128)}) custom-call(bf16[128,512]{1,0:T(8,128)(2,1)} %q_hbm.1, bf16[128,128]{1,0:T(8,128)(2,1)} %k_hbm.1, bf16[128,128]{1,0:T(8,128)(2,1)} %v_hbm.1, bf16[128,512]{1,0:T(8,128)(2,1)} %g_hbm.1, s32[16,16]{1,0:T(8,128)} %mask_ref.1, ...), custom_call_target="tpu_custom_call" | custom-call | tf_op jit(solution)/shard_map/pallas_call | solution.py:291
  33.2 1.7 %shard_map.94 = (bf16[128,512]{1,0:T(8,128)(2,1)}, bf16[128,512]{1,0:T(8,128)(2,1)}, f32[128,128]{1,0:T(8,128)}, f32[128,128]{1,0:T(8,128)}) custom-call(bf16[128,512]{1,0:T(8,128)(2,1)} %get-tuple-element.8.refs_0_, bf16[128,512]{1,0:T(8,128)(2,1)} %get-tuple-element.9.refs_1_, f32[128,128]{1,0:T(8,128)} %get-tuple-element.10.refs_2_, ...), custom_call_target="tpu_custom_call" | custom-call | tf_op jit(solution)/shard_map/pallas_call | solution.py:321

commit v3 on v2

--- a/solution.py
+++ b/solution.py
@@ -12,7 +12,6 @@
 F32 = jnp.float32
 BF16 = jnp.bfloat16
 MASKED = -1e30
-VMEM_BYTES = 58 * 1024 * 1024
 
 
 def dot(a, b):
@@ -20,8 +19,8 @@
 
 
 def kernel(
-    n, q_hbm, k_hbm, v_hbm, g_hbm, mask_ref, order_ref, att_ref, dq_ref, dk_ref, dv_ref,
-    q_ref, g_ref, kv, qr, qt, gr, gt, prob, dprob, maxes, acc, send_a, recv_a, send_b, recv_b, send_c, recv_c,
+    n, q_hbm, k_hbm, v_hbm, g_hbm, mask_hbm, order_hbm, att_ref, dq_ref, dk_ref, dv_ref,
+    mask_ref, order_ref, q_ref, g_ref, kv, qr, qt, gr, gt, prob, dprob, maxes, acc, send_a, recv_a, send_b, recv_b, send_c, recv_c,
     in_s, gz_s, gz_r, gy_s, gy_r, gc_s, gc_r, a_s, a_r, b_s, b_r, c_s, c_r,
 ):
     m = n // 4
@@ -83,7 +82,8 @@
     loads = [
         pltpu.make_async_copy(src, dst, in_s.at[i])
         for i, (src, dst) in enumerate(
-            [(k_hbm, kv.at[KEY, 0, 0, 0]), (v_hbm, kv.at[VALUE, 0, 0, 0]), (q_hbm, q_ref), (g_hbm, g_ref)]
+            [(k_hbm, kv.at[KEY, 0, 0, 0]), (v_hbm, kv.at[VALUE, 0, 0, 0]), (q_hbm, q_ref), (g_hbm, g_ref),
+             (mask_hbm, mask_ref), (order_hbm, order_ref)]
         )
     ]
     for load in loads:
@@ -260,13 +260,9 @@
 
 
 def write_out(*refs):
-    ins, outs, held, in_s, out_s = refs[:4], refs[4:8], refs[8:12], refs[12], refs[13]
-    loads = [pltpu.make_async_copy(ins[i], held[i], in_s.at[i]) for i in range(4)]
-    stores = [pltpu.make_async_copy(held[i], outs[i], out_s.at[i]) for i in range(4)]
-    for load in loads:
-        load.start()
-    for load, store in zip(loads, stores):
-        load.wait()
+    out_s = refs[8]
+    stores = [pltpu.make_async_copy(refs[i], refs[4 + i], out_s.at[i]) for i in range(4)]
+    for store in stores:
         store.start()
     for store in stores:
         store.wait()
@@ -278,9 +274,8 @@
     tok, hd = key_states.shape
     rows = queries.shape[1] // hd * tok
     assert n == 4 * m and tile_mask.shape[1] == n
-    hbm = pl.BlockSpec(memory_space=pl.ANY)
+    hbm = pl.BlockSpec(memory_space=pltpu.HBM)
     vmem = pl.BlockSpec(memory_space=pltpu.VMEM)
-    smem = pl.BlockSpec(memory_space=pltpu.SMEM)
     dma = pltpu.SemaphoreType.DMA
     shapes = (
         jax.ShapeDtypeStruct(queries.shape, BF16),
@@ -290,10 +285,12 @@
     )
     results = pl.pallas_call(
         functools.partial(kernel, n),
-        out_shape=shapes,
-        in_specs=[hbm] * 4 + [smem] * 2,
+        out_shape=tuple(pltpu.VMEM(s.shape, s.dtype) for s in shapes),
+        in_specs=[hbm] * 6,
         out_specs=(vmem,) * 4,
         scratch_shapes=[
+            pltpu.SMEM(tile_mask.shape, jnp.int32),
+            pltpu.SMEM(block_order.shape, jnp.int32),
             pltpu.VMEM(queries.shape, BF16),
             pltpu.VMEM(queries.shape, BF16),
             pltpu.VMEM((2, m, 2, 2, tok, hd), BF16),
@@ -311,20 +308,20 @@
             pltpu.VMEM((2, m, tok, hd), BF16),
             pltpu.VMEM((2, m, tok, hd), BF16),
             pltpu.VMEM((2, m, tok, hd), BF16),
-            dma((4,)), dma((2, m)), dma((2, m)), dma((2, m)), dma((2, m)), dma((2, m, 2)), dma((2, m, 2)),
+            dma((6,)), dma((2, m)), dma((2, m)), dma((2, m)), dma((2, m)), dma((2, m, 2)), dma((2, m, 2)),
             dma((2, m)), dma((2, m)), dma((2, m)), dma((2, m)), dma((2, m)), dma((2, m)),
         ],
         compiler_params=pltpu.CompilerParams(
-            collective_id=0, has_side_effects=True, vmem_limit_bytes=VMEM_BYTES
+            collective_id=0, has_side_effects=True, vmem_limit_bytes=58 * 1024 * 1024
         ),
     )(queries, key_states, value_states, grad_out, tile_mask, block_order)
     return pl.pallas_call(
         write_out,
         out_shape=shapes,
-        in_specs=[hbm] * 4,
+        in_specs=[vmem] * 4,
         out_specs=(hbm,) * 4,
-        scratch_shapes=[pltpu.VMEM(s.shape, s.dtype) for s in shapes] + [dma((4,)), dma((4,))],
-        compiler_params=pltpu.CompilerParams(vmem_limit_bytes=VMEM_BYTES),
+        scratch_shapes=[dma((4,))],
+        compiler_params=pltpu.CompilerParams(vmem_limit_bytes=8 * 1024 * 1024),
     )(*results)
 
 

time: 35.1 us -> 32.7 us (0.932)
  Pallas kernels: 34.3 us -> 32 us
    pallas_call x2, Pallas kernels: 34.3 us -> 32 us  [the longest x1 31.2 us: shards(): pl.pallas_call(functools.partial(kernel, n), out_shape=tuple((pltpu.VMEM(...]
where the time goes in v3:
time: 32.7 us; the launch traced here: 32.6 us
  Pallas kernels  32 us (98%)
  between operations  0.64 us (2%)
    pallas_call x1, Pallas kernels, shards(): pl.pallas_call(functools.partial(kernel, n), out_shape=tuple((pltpu.VMEM(...  31.2 us
    pallas_call x1, Pallas kernels, shards(): pl.pallas_call(write_out, out_shape=shapes, in_specs=[vmem] * 4, out_spec...  0.77 us

profile of v3, /device:TPU:0, one launch (start us, length us, event | category | flops | bytes accessed | tf_op | source)
XLA Modules:
  0.0 32.6 jit_solution(3699870186294157849)
XLA Ops:
  0.6 31.2 %shard_map.93 = (bf16[128,512]{1,0:T(8,128)(2,1)S(1)}, bf16[128,512]{1,0:T(8,128)(2,1)S(1)}, f32[128,128]{1,0:T(8,128)S(1)}, f32[128,128]{1,0:T(8,128)S(1)}) custom-call(bf16[128,512]{1,0:T(8,128)(2,1)} %q_hbm.1, bf16[128,128]{1,0:T(8,128)(2,1)} %k_hbm.1, bf16[128,128]{1,0:T(8,128)(2,1)} %v_hbm.1, bf16[128,512]{1,0:T(8,128)(2,1)} %g_hbm.1, ...), custom_call_target="tpu_custom_call" | custom-call | tf_op jit(solution)/shard_map/pallas_call | solution.py:286
  31.8 0.8 %shard_map.94 = (bf16[128,512]{1,0:T(8,128)(2,1)}, bf16[128,512]{1,0:T(8,128)(2,1)}, f32[128,128]{1,0:T(8,128)}, f32[128,128]{1,0:T(8,128)}) custom-call(bf16[128,512]{1,0:T(8,128)(2,1)S(1)} %get-tuple-element.8.refs_0_, bf16[128,512]{1,0:T(8,128)(2,1)S(1)} %get-tuple-element.9.refs_1_, f32[128,128]{1,0:T(8,128)S(1)} %get-tuple-element.10.refs_2_, ...), custom_call_target="tpu_custom_call" | custom-call | tf_op jit(solution)/shard_map/pallas_call | solution.py:318
